TPU v7x, 256 devices: a whole 4x4x8 slice. The times are simulated.
256 devices in a mesh: noise: 8 (over x, core), sample: 32 (over y, z).
Axes of the slice: x: 4, y: 4, z: 8, core: 2. Of those that a mesh axis runs over, the one named last changes fastest.
Arguments:
- noise_latents: bfloat16 [16384, 256], P(('noise', 'sample')), may hold values from -18 to 18
- teacher_latent_rows: bfloat16 [32768, 256], P('sample', 'noise'), may hold values from -6 to 6
Outputs:
- noise_row_potential: float32 [16384], P('noise')
- column_potential: float32 [32768], P('sample')
- targets: bfloat16 [16384, 256], P(('noise', 'sample'))
All inputs are finite; a program needn't handle non-finite values.
Results may differ from a plain program's by a relative error of at most 0.0039.
Values may be sent and summed in bfloat16 or wider, within the bound.
A program may use at most 64 MiB of HBM per device.

v0:
```python
import math

import jax
import jax.numpy as jnp
from jax import lax
from jax.sharding import PartitionSpec as P

ITERS = 3


smoothing_strength = 0.1


def source_logsumexp_partial(scores):
    local_peak = jnp.max(scores, axis=1)
    peak = lax.pmax(local_peak, "sample")
    total = lax.psum(jnp.sum(jnp.exp(scores - peak[:, None]), axis=1), "sample")
    return peak + jnp.log(total)


def col_lse(scores):
    local_peak = jnp.max(scores, axis=0)
    peak = lax.pmax(local_peak, "noise")
    total = lax.psum(jnp.sum(jnp.exp(scores - peak[None, :]), axis=0), "noise")
    return peak + jnp.log(total)


def shards(noise_latents, teacher_latent_rows):
    rows_x = lax.all_gather(noise_latents, "sample", axis=0, tiled=True)
    cols_y = lax.all_gather(teacher_latent_rows, "noise", axis=1, tiled=True)
    embed_dimension = rows_x.shape[1]
    multiplier_coefficient = 1.0 / (embed_dimension * smoothing_strength)
    row_count = rows_x.shape[0]
    col_count = cols_y.shape[0]
    total_rows = row_count * lax.axis_size("noise")
    overall_destination_number = col_count * lax.axis_size("sample")
    xn = jnp.sum(rows_x.astype(jnp.float32) ** 2, axis=1)
    yn = jnp.sum(cols_y.astype(jnp.float32) ** 2, axis=1)

    def kernel():
        inner = jnp.dot(rows_x, cols_y.T, preferred_element_type=jnp.float32)
        return (xn[:, None] + yn[None, :] - 2.0 * inner) * multiplier_coefficient

    def cost():
        return kernel()

    column_potential = jnp.zeros((col_count,), jnp.float32)
    noise_row_potential = jnp.zeros((row_count,), jnp.float32)
    for step in range(ITERS):
        noise_row_potential = -math.log(total_rows) - source_logsumexp_partial(
            column_potential[None, :] - cost()
        )
        column_potential = -math.log(overall_destination_number) - col_lse(
            noise_row_potential[:, None] - cost()
        )
    plan = jnp.exp(noise_row_potential[:, None] + column_potential[None, :] - cost())
    mass_part = jnp.sum(plan, axis=1)
    numer = jnp.dot(plan.astype(jnp.bfloat16), cols_y, preferred_element_type=jnp.float32)
    numer_all, mass_all = lax.psum((numer, mass_part), "sample")
    share = row_count // lax.axis_size("sample")
    start = lax.axis_index("sample") * share
    numer_own = lax.dynamic_slice_in_dim(numer_all, start, share, 0)
    mass_own = lax.dynamic_slice_in_dim(mass_all, start, share, 0)
    targets = (numer_own / mass_own[:, None]).astype(jnp.bfloat16)
    return (noise_row_potential, column_potential, targets)


def solution(mesh):
    placed = (P(("noise", "sample"), None), P("sample", "noise"))
    return jax.shard_map(
        shards,
        mesh=mesh,
        in_specs=placed,
        out_specs=(P("noise"), P("sample"), P(("noise", "sample"), None)),
        check_vma=False,
    )
```

profile of v0, /device:TPU:1, one launch (start us, length us, event | category | flops | bytes accessed | tf_op | source)
XLA Modules:
  0.0 807.6 jit_solution(9159708319463455959)
XLA Ops:
  7.9 16.4 %all_gather.7 = bf16[1024,256]{0,1:T(8,128)(2,1)S(1)} all-gather(bf16[1024,32]{0,1:T(8,128)(2,1)} %param.3), channel_id=1, replica_groups=mesh['noise'=8,'sample'=32] {'noise'}, dimensions={1}, use_global_device_ids=true | all-gather | bytes 589824 | tf_op jit(solution)/shard_map/all_gather | solution.py:30
  24.5 61.7 %all-gather.2.cloned.1.call-done = bf16[2048,256]{1,0:T(8,128)(2,1)} async-done(((bf16[64,256]{1,0:T(8,128)(2,1)}), bf16[2048,256]{1,0:T(8,128)(2,1)}) %all-gather.2.cloned.1.call-update) | async-done | bytes 1048592 | tf_op jit(solution)/shard_map/all_gather | solution.py:29
  87.8 5.6 subtract_reduce_fusion.5
  93.3 59.0 %pmax.42 = f32[2048]{0:T(1024)S(1)} all-reduce(f32[2048]{0:T(1024)S(1)} %get-tuple-element.3), channel_id=1, replica_groups=mesh['noise'=8,'sample'=32] {'sample'}, use_global_device_ids=true, to_apply=%region_3.0 | all-reduce | flops 2048 | bytes 16384 | tf_op jit(solution)/shard_map/pmax | solution.py:16
  152.4 4.8 exponential_reduce_fusion.5
  157.1 57.1 %psum.56 = f32[2048]{0:T(1024)S(1)} all-reduce(f32[2048]{0:T(1024)S(1)} %exponential_reduce_fusion.5), channel_id=1, replica_groups=mesh['noise'=8,'sample'=32] {'sample'}, use_global_device_ids=true, to_apply=%region_5.0 | all-reduce | flops 2048 | bytes 16384 | tf_op jit(solution)/shard_map/psum | solution.py:17
  218.3 44.8 %pmax.43 = f32[1024]{0:T(1024)S(1)} all-reduce(f32[1024]{0:T(1024)S(1)} %subtract_reduce_fusion.4), channel_id=1, replica_groups=mesh['noise'=8,'sample'=32] {'noise'}, use_global_device_ids=true, to_apply=%region_7.0 | all-reduce | flops 1024 | bytes 8192 | tf_op jit(solution)/shard_map/pmax | solution.py:23
  263.0 4.4 exponential_reduce_fusion.4
  267.4 12.4 %psum.57 = f32[1024]{0:T(1024)S(1)} all-reduce(f32[1024]{0:T(1024)S(1)} %exponential_reduce_fusion.4), channel_id=1, replica_groups=mesh['noise'=8,'sample'=32] {'noise'}, use_global_device_ids=true, to_apply=%region_9.0 | all-reduce | flops 1024 | bytes 8192 | tf_op jit(solution)/shard_map/psum | solution.py:24
  283.8 58.4 %pmax.44 = f32[2048]{0:T(1024)S(1)} all-reduce(f32[2048]{0:T(1024)S(1)} %subtract_reduce_fusion.3), channel_id=1, replica_groups=mesh['noise'=8,'sample'=32] {'sample'}, use_global_device_ids=true, to_apply=%region_11.0 | all-reduce | flops 2048 | bytes 16384 | tf_op jit(solution)/shard_map/pmax | solution.py:16
  342.2 4.3 exponential_reduce_fusion.3
  346.6 56.8 %psum.58 = f32[2048]{0:T(1024)S(1)} all-reduce(f32[2048]{0:T(1024)S(1)} %exponential_reduce_fusion.3), channel_id=1, replica_groups=mesh['noise'=8,'sample'=32] {'sample'}, use_global_device_ids=true, to_apply=%region_13.0 | all-reduce | flops 2048 | bytes 16384 | tf_op jit(solution)/shard_map/psum | solution.py:17
  407.4 40.5 %pmax.45 = f32[1024]{0:T(1024)S(1)} all-reduce(f32[1024]{0:T(1024)S(1)} %subtract_reduce_fusion.2), channel_id=1, replica_groups=mesh['noise'=8,'sample'=32] {'noise'}, use_global_device_ids=true, to_apply=%region_15.0 | all-reduce | flops 1024 | bytes 8192 | tf_op jit(solution)/shard_map/pmax | solution.py:23
  447.9 4.4 exponential_reduce_fusion.2
  452.3 12.4 %psum.59 = f32[1024]{0:T(1024)S(1)} all-reduce(f32[1024]{0:T(1024)S(1)} %exponential_reduce_fusion.2), channel_id=1, replica_groups=mesh['noise'=8,'sample'=32] {'noise'}, use_global_device_ids=true, to_apply=%region_17.0 | all-reduce | flops 1024 | bytes 8192 | tf_op jit(solution)/shard_map/psum | solution.py:24
  468.7 58.4 %pmax.46 = f32[2048]{0:T(1024)S(1)} all-reduce(f32[2048]{0:T(1024)S(1)} %subtract_reduce_fusion.1), channel_id=1, replica_groups=mesh['noise'=8,'sample'=32] {'sample'}, use_global_device_ids=true, to_apply=%region_19.0 | all-reduce | flops 2048 | bytes 16384 | tf_op jit(solution)/shard_map/pmax | solution.py:16
  527.1 4.3 exponential_reduce_fusion.1
  531.4 57.0 %psum.60 = f32[2048]{0:T(1024)S(1)} all-reduce(f32[2048]{0:T(1024)S(1)} %exponential_reduce_fusion.1), channel_id=1, replica_groups=mesh['noise'=8,'sample'=32] {'sample'}, use_global_device_ids=true, to_apply=%region_21.0 | all-reduce | flops 2048 | bytes 16384 | tf_op jit(solution)/shard_map/psum | solution.py:17
  592.5 40.5 %pmax.47 = f32[1024]{0:T(1024)S(1)} all-reduce(f32[1024]{0:T(1024)S(1)} %subtract_reduce_fusion), channel_id=1, replica_groups=mesh['noise'=8,'sample'=32] {'noise'}, use_global_device_ids=true, to_apply=%region_23.0 | all-reduce | flops 1024 | bytes 8192 | tf_op jit(solution)/shard_map/pmax | solution.py:23
  633.0 4.4 exponential_reduce_fusion
  637.4 12.4 %psum.61 = f32[1024]{0:T(1024)S(1)} all-reduce(f32[1024]{0:T(1024)S(1)} %exponential_reduce_fusion), channel_id=1, replica_groups=mesh['noise'=8,'sample'=32] {'noise'}, use_global_device_ids=true, to_apply=%region_25.0 | all-reduce | flops 1024 | bytes 8192 | tf_op jit(solution)/shard_map/psum | solution.py:24
  649.8 6.5 fusion.2
  660.6 58.5 %psum.63 = f32[2048]{0:T(1024)S(1)} all-reduce(f32[2048]{0:T(1024)S(1)} %fusion), channel_id=1, replica_groups=mesh['noise'=8,'sample'=32] {'sample'}, use_global_device_ids=true, to_apply=%region_28.0 | all-reduce | flops 2048 | bytes 16384 | tf_op jit(solution)/shard_map/psum | solution.py:59
  719.2 80.0 %all-reduce.2.cloned.1.call-done = f32[2048,256]{1,0:T(8,128)} async-done(((f32[2048,256]{1,0:T(8,128)}), f32[2048,256]{1,0:T(8,128)}) %all-reduce.2.cloned.1.call-update) | async-done | bytes 2097168 | tf_op jit(solution)/shard_map/psum | solution.py:59
  (24 shorter events, 28.5 us)
Async XLA Ops:
  7.2 79.0 %all-gather.2.cloned.1.call-start = ((), (), s32[]{:S(2)}) async-start(), calls=%async_computation | async-start | bytes 1081344 | tf_op jit(solution)/shard_map/all_gather | solution.py:29
  7.9 791.3 %all-reduce.2.cloned.1.call-start = ((), (), s32[]{:S(2)}) async-start(), calls=%async_computation.1 | async-start | bytes 4194304 | tf_op jit(solution)/shard_map/psum | solution.py:59
  588.5 67.8 %copy-start = (f32[2048]{0:T(1024)}, f32[2048]{0:T(1024)S(1)}, u32[]{:S(2)}) copy-start(f32[2048]{0:T(1024)S(1)} %add_subtract_fusion) | copy-start | bytes 24580
  649.8 6.5 copy-start.1
Sparse Core Ops, SparseCore 0:
  10.6 75.5 all-gather.1
  656.4 142.7 all-reduce.1
where the time goes:
time: 812 us; the launch traced here: 808 us
  blocking collectives  585 us (72%)
  waiting for transfers between devices  142 us (17%)
  other arithmetic  54.1 us (7%)
  between operations  14.2 us (2%)
  matrix products  12 us (1%)
    pmax x3, blocking collectives, source_logsumexp_partial(): peak = lax.pmax(local_peak, 'sample')  176 us
    psum x3, blocking collectives, source_logsumexp_partial(): total = lax.psum(jnp.sum(jnp.exp(scores - peak[:, None]), axis=1), 'sample')  171 us
    pmax x3, blocking collectives, col_lse(): peak = lax.pmax(local_peak, 'noise')  126 us
    psum x1, waiting for transfers between devices, shards(): numer_all, mass_all = lax.psum((numer, mass_part), 'sample')  80 us
    all_gather x1, waiting for transfers between devices, shards(): rows_x = lax.all_gather(noise_latents, 'sample', axis=0, tiled=True)  61.7 us
    psum x1, blocking collectives, shards(): numer_all, mass_all = lax.psum((numer, mass_part), 'sample')  58.5 us
    psum x3, blocking collectives, col_lse(): total = lax.psum(jnp.sum(jnp.exp(scores - peak[None, :]), axis=0), 'noise')  37.3 us
    all_gather x1, blocking collectives, shards(): cols_y = lax.all_gather(teacher_latent_rows, 'noise', axis=1, tiled=True)  16.4 us
  transfers between devices with their start and end apart: 2, of which 2 were waited for; matrix products, arithmetic and copies ran while one was open for 1% of the time, Pallas kernels for 0%

commit v1 on v0

v1 whole, which is shorter than its diff:
```python
import functools
import math

import jax
import jax.numpy as jnp
from jax import lax
from jax.experimental import pallas as pl
from jax.experimental.pallas import tpu as pltpu
from jax.sharding import PartitionSpec as P

ITERS = 3
WIDTH = 256
ROWS, COLS = 16384, 32768
STRENGTH = 0.1
NX, NY, NZ, NC = 4, 4, 8, 2
GROUP = 16
SHARE = 64
BLOCK_ROWS = GROUP * SHARE
PIECE = 256
CUT = 128
CUTS = BLOCK_ROWS // CUT
TILES = NZ * PIECE // 128
MESH = pl.DeviceIdType.MESH
F32, BF16 = jnp.float32, jnp.bfloat16
LN2 = math.log(2.0)
COST = 1.0 / (WIDTH * STRENGTH)


def place(x, c, y, z):
    return (x * NC + c, y * NZ + z)


def spread(row):
    return jnp.broadcast_to(row, (128, 128)).T


def kernel(noise_ref, teach_ref, row_out, col_out, target_out, slices, cols, rows_x, tall, score, peak, total,
           gain, beta, plan, row_box, col_box, row_pot, col_pot, mine, boxes,
           sa, ra, sx, rx, sz, rz, sc, rc, srow, rrow, scol, rcol, sn, rn, so, ro, sp, rp):
    n, s = lax.axis_index("noise"), lax.axis_index("sample")
    x, c = n // NC, n % NC
    y, z = s // NZ, s % NZ
    me = x * NY + y
    other = 1 - c
    slot = z * NC + c

    def xy(k):
        px, py = (x + k // NY) % NX, (y + k % NY) % NY
        return px * NY + py, place(px, c, py, z)

    def zc(k):
        pz, pc = (z + k // NC) % NZ, (c + k % NC) % NC
        return pz * NC + pc, place(x, pc, y, pz)

    barrier = pltpu.get_barrier_semaphore()

    def greet(k, carry):
        pl.semaphore_signal(barrier, inc=1, device_id=xy(k)[1], device_id_type=MESH)
        pl.semaphore_signal(barrier, inc=1, device_id=zc(k)[1], device_id_type=MESH)
        return carry

    lax.fori_loop(1, GROUP, greet, 0)

    row_id = lax.broadcasted_iota(jnp.int32, (32, 32), 0)
    col_id = lax.broadcasted_iota(jnp.int32, (32, 32), 1)
    eye = jnp.where(row_id == col_id, 1.0, 0.0).astype(BF16)
    for q in range(NX):
        part = lax.dot_general(eye, teach_ref[q * PIECE:(q + 1) * PIECE, :], (((1,), (1,)), ((), ())),
                               preferred_element_type=F32)
        slices[q] = part.astype(BF16)
    rows_x[me] = noise_ref[...]
    cols[z, x, c] = slices[x]

    pl.semaphore_wait(barrier, 2 * (GROUP - 1))

    def quarter(k):
        px = (x + k) % NX
        return px, pltpu.make_async_remote_copy(
            src_ref=slices.at[px], dst_ref=cols.at[z, x, c], send_sem=sa.at[px], recv_sem=ra.at[x],
            device_id=place(px, c, y, z), device_id_type=MESH)

    def quarter_in(k):
        px = (x + k) % NX
        return pltpu.make_async_remote_copy(
            src_ref=slices.at[px], dst_ref=cols.at[z, px, c], send_sem=sa.at[px], recv_sem=ra.at[px],
            device_id=place(px, c, y, z), device_id_type=MESH)

    for k in range(1, NX):
        quarter(k)[1].start()

    def noise_copy(k, incoming):
        p, device = xy(k)
        at = p if incoming else me
        return pltpu.make_async_remote_copy(
            src_ref=rows_x.at[me], dst_ref=rows_x.at[at], send_sem=sx.at[p], recv_sem=rx.at[at],
            device_id=device, device_id_type=MESH)

    def noise_start(k, carry):
        noise_copy(k, False).start()
        return carry

    lax.fori_loop(1, GROUP, noise_start, 0)
    for k in range(1, NX):
        quarter_in(k).wait_recv()

    def piece_copy(d, incoming):
        pz = (z + d) % NZ
        at = pz if incoming else z
        return pltpu.make_async_remote_copy(
            src_ref=cols.at[z, :, c], dst_ref=cols.at[at, :, c], send_sem=sz.at[pz], recv_sem=rz.at[at],
            device_id=place(x, c, y, pz), device_id_type=MESH)

    def core_copy(pz, incoming):
        at = other if incoming else c
        return pltpu.make_async_remote_copy(
            src_ref=cols.at[pz, :, c], dst_ref=cols.at[pz, :, at], send_sem=sc.at[pz], recv_sem=rc.at[pz],
            device_id=place(x, other, y, z), device_id_type=MESH)

    def away(k):
        return ((k + 1) // 2) * (2 * (k % 2) - 1) + NZ

    def piece_start(k, carry):
        piece_copy(away(k) % NZ, False).start()
        return carry

    lax.fori_loop(1, NZ, piece_start, 0)

    peak[...] = jnp.full((BLOCK_ROWS, 128), -1e30, F32)
    total[...] = jnp.zeros((BLOCK_ROWS, 128), F32)

    def noise_wait(k, carry):
        noise_copy(k, True).wait_recv()
        return carry

    lax.fori_loop(1, GROUP, noise_wait, 0)

    def scores_of(pz):
        block = cols[pz].reshape(WIDTH, PIECE)
        wide = block.astype(F32)
        norms = jnp.sum(wide * wide, axis=0, keepdims=True) * (COST / LN2)
        for b in range(CUTS):
            r = pl.ds(b * CUT, CUT)
            latents = rows_x[2 * b:2 * b + 2].reshape(CUT, WIDTH)
            dots = jnp.dot(latents, block, preferred_element_type=F32)
            h = dots * (2.0 * COST / LN2) - norms
            score[pz, r, :] = h
            left, right = h[:, :128], h[:, 128:]
            old = peak[r, :]
            new = jnp.maximum(old, jnp.maximum(left, right))
            total[r, :] = total[r, :] * jnp.exp2(old - new) + (jnp.exp2(left - new) + jnp.exp2(right - new))
            peak[r, :] = new

    def piece(k, carry):
        @pl.when(k < NZ)
        def _():
            d = away(k) % NZ
            pz = (z + d) % NZ

            @pl.when(k > 0)
            def _():
                piece_copy(d, True).wait_recv()

            core_copy(pz, False).start()

        @pl.when(k > 0)
        def _():
            pz = (z + away(k - 1)) % NZ
            core_copy(pz, True).wait_recv()
            scores_of(pz)

        return carry

    lax.fori_loop(0, NZ + 1, piece, 0)

    def row_copy(turn, k, incoming):
        p, device = xy(k)
        at = p if incoming else me
        return pltpu.make_async_remote_copy(
            src_ref=row_box.at[turn, me], dst_ref=row_box.at[turn, at], send_sem=srow.at[turn, p],
            recv_sem=rrow.at[turn, at], device_id=device, device_id_type=MESH)

    def row_start(turn):
        def start(k, carry):
            row_copy(turn, k, False).start()
            return carry

        lax.fori_loop(1, GROUP, start, 0)

    def row_wait(turn):
        def wait(k, carry):
            row_copy(turn, k, True).wait_recv()
            return carry

        lax.fori_loop(1, GROUP, wait, 0)

    def col_copy(turn, k, incoming):
        p, device = zc(k)
        at = p if incoming else slot
        return pltpu.make_async_remote_copy(
            src_ref=col_box.at[turn, slot], dst_ref=col_box.at[turn, at], send_sem=scol.at[turn, p],
            recv_sem=rcol.at[turn, at], device_id=device, device_id_type=MESH)

    def col_trade(turn):
        def start(k, carry):
            col_copy(turn, k, False).start()
            return carry

        lax.fori_loop(1, GROUP, start, 0)

        def wait(k, carry):
            col_copy(turn, k, True).wait_recv()
            return carry

        lax.fori_loop(1, GROUP, wait, 0)

    for b in range(CUTS):
        r = pl.ds(b * CUT, CUT)
        lane_peak = peak[r, :].T
        lane_total = total[r, :].T
        top = jnp.max(lane_peak, axis=0, keepdims=True)
        sums = jnp.sum(lane_total * jnp.exp2(lane_peak - top), axis=0, keepdims=True)
        row_box[0, me, b:b + 1, :] = top + jnp.log(sums) * (1.0 / LN2)
    row_start(0)
    for pz in range(NZ):
        block = cols[pz].reshape(WIDTH, PIECE).astype(F32)
        tall[pz * PIECE:(pz + 1) * PIECE, :] = block.T.astype(BF16)
    for b in range(CUTS):
        latents = rows_x[2 * b:2 * b + 2].reshape(CUT, WIDTH).astype(F32)
        squares = latents * latents
        mine[0, b:b + 1, :] = jnp.sum((squares[:, :128] + squares[:, 128:]).T, axis=0, keepdims=True)
    row_wait(0)
    lse = row_box[0]
    top = jnp.max(lse, axis=0)
    row_log = -math.log2(ROWS) - (top + jnp.log(jnp.sum(jnp.exp2(lse - top), axis=0)) * (1.0 / LN2))

    mine[1] = row_log

    def first_column(b, carry):
        r = pl.ds(pl.multiple_of(b * CUT, CUT), CUT)
        shift = spread(mine[1, pl.ds(b, 1), :])
        for t in range(TILES):
            lanes = pl.ds((t % 2) * 128, 128)
            h = score[t // 2, r, lanes] + shift
            top = jnp.max(h, axis=0, keepdims=True)
            e = jnp.exp2(h - top)
            score[t // 2, r, lanes] = e
            gain[b, t:t + 1, :] = top
            beta[b, t:t + 1, :] = jnp.sum(e, axis=0, keepdims=True)
        return carry

    lax.fori_loop(0, CUTS, first_column, 0)
    cut_peak = gain[...]
    top = jnp.max(cut_peak, axis=0)
    sums = jnp.sum(beta[...] * jnp.exp2(cut_peak - top), axis=0)
    col_box[0, slot] = top + jnp.log(sums) * (1.0 / LN2)
    col_trade(0)
    lse = col_box[0]
    top = jnp.max(lse, axis=0)
    col_log = -math.log2(COLS) - (top + jnp.log(jnp.sum(jnp.exp2(lse - top), axis=0)) * (1.0 / LN2))
    gain[...] = jnp.exp2(cut_peak + col_log)
    beta[...] = gain[...]

    alpha = None
    for turn in range(1, ITERS):
        def row_sums(b, carry):
            r = pl.ds(pl.multiple_of(b * CUT, CUT), CUT)
            acc = None
            for t in range(TILES):
                term = score[t // 2, r, (t % 2) * 128:(t % 2) * 128 + 128] * beta[b, t:t + 1, :]
                acc = term if acc is None else acc + term
            row_box[turn, me, pl.ds(b, 1), :] = jnp.sum(acc.T, axis=0, keepdims=True)
            return carry

        lax.fori_loop(0, CUTS, row_sums, 0)
        row_start(turn)
        row_wait(turn)
        alpha = 1.0 / (ROWS * jnp.sum(row_box[turn], axis=0))
        mine[2] = alpha

        def col_sums(b, carry):
            r = pl.ds(pl.multiple_of(b * CUT, CUT), CUT)
            weight = spread(mine[2, pl.ds(b, 1), :])
            out = []
            for t in range(TILES):
                term = score[t // 2, r, (t % 2) * 128:(t % 2) * 128 + 128] * weight
                out.append(carry[t] + jnp.sum(term.reshape(CUT // 8, 8, 128), axis=0) * gain[b, t:t + 1, :])
            return tuple(out)

        sums = lax.fori_loop(0, CUTS, col_sums, tuple(jnp.zeros((8, 128), F32) for _ in range(TILES)))
        for t in range(TILES):
            col_box[turn, slot, t:t + 1, :] = jnp.sum(sums[t], axis=0, keepdims=True)
        col_trade(turn)
        factor = 1.0 / (COLS * jnp.sum(col_box[turn], axis=0))
        beta[...] = gain[...] * factor

    row_pot[z] = COST * mine[0] + LN2 * (row_log + jnp.log(alpha) * (1.0 / LN2))
    col_pot[x] = LN2 * (col_log + jnp.log(factor) * (1.0 / LN2))

    def row_pot_copy(d, incoming):
        pz = (z + d) % NZ
        at = pz if incoming else z
        return pltpu.make_async_remote_copy(
            src_ref=row_pot.at[z], dst_ref=row_pot.at[at], send_sem=so.at[pz], recv_sem=ro.at[at],
            device_id=place(x, c, y, pz), device_id_type=MESH)

    def col_pot_copy(d, incoming):
        px = (x + d) % NX
        at = px if incoming else x
        return pltpu.make_async_remote_copy(
            src_ref=col_pot.at[x], dst_ref=col_pot.at[at], send_sem=sp.at[px], recv_sem=rp.at[at],
            device_id=place(px, c, y, z), device_id_type=MESH)

    def row_pot_start(d, carry):
        row_pot_copy(d, False).start()
        return carry

    def col_pot_start(d, carry):
        col_pot_copy(d, False).start()
        return carry

    lax.fori_loop(1, NZ, row_pot_start, 0)
    lax.fori_loop(1, NX, col_pot_start, 0)

    def sum_copy(p, device, incoming):
        at = p if incoming else me
        return pltpu.make_async_remote_copy(
            src_ref=boxes.at[0, p], dst_ref=boxes.at[1, at], send_sem=sn.at[p], recv_sem=rn.at[at],
            device_id=device, device_id_type=MESH)

    def project(step, carry):
        px = (x + 1 + step) % NX
        for half in range(2):
            b = px * 2 + half
            r = pl.ds(pl.multiple_of(b * CUT, CUT), CUT)
            weight = spread(mine[2, pl.ds(b, 1), :])
            acc = None
            for t in range(TILES):
                p = score[t // 2, r, (t % 2) * 128:(t % 2) * 128 + 128] * weight * beta[b, t:t + 1, :]
                acc = p if acc is None else acc + p
                plan[half * CUT:half * CUT + CUT, t * 128:t * 128 + 128] = p.astype(BF16)
            row_box[ITERS, me, pl.ds(b, 1), :] = jnp.sum(acc.T, axis=0, keepdims=True)
        numer = jnp.dot(plan[...], tall[...], preferred_element_type=F32).astype(BF16)
        for py in range(NY):
            p = px * NY + py
            boxes[0, p] = numer[py * SHARE:(py + 1) * SHARE, :]

            @pl.when(p != me)
            def _():
                sum_copy(p, place(px, c, py, z), False).start()

        return carry

    lax.fori_loop(0, NX, project, 0)
    row_start(ITERS)
    boxes[1, me] = boxes[0, me]

    def col_pot_wait(d, carry):
        col_pot_copy(d, True).wait_recv()
        return carry

    def row_pot_wait(d, carry):
        row_pot_copy(d, True).wait_recv()
        return carry

    lax.fori_loop(1, NX, col_pot_wait, 0)
    for px in range(NX):
        for half in range(2):
            col_out[2 * px + half:2 * px + half + 1, :] = col_pot[px, pl.ds(2 * z + half, 1), :]
    lax.fori_loop(1, NZ, row_pot_wait, 0)
    low = lax.broadcasted_iota(jnp.int32, (1, 128), 1) < SHARE
    for py in range(NY):
        for pair in range(NZ // 2):
            even = row_pot[2 * pair, pl.ds(2 * x + py // 2, 1), :]
            odd = row_pot[2 * pair + 1, pl.ds(2 * x + py // 2, 1), :]
            if py % 2:
                even = pltpu.roll(even, SHARE, 1)
            else:
                odd = pltpu.roll(odd, SHARE, 1)
            row_out[4 * py + pair:4 * py + pair + 1, :] = jnp.where(low, even, odd)

    row_wait(ITERS)
    mine[3] = jnp.sum(row_box[ITERS], axis=0)
    total[0:128, :] = spread(mine[3, pl.ds(me // 2, 1), :])
    mass = total[pl.ds(pl.multiple_of((me % 2) * SHARE, SHARE), SHARE), :]

    def sum_wait(k, carry):
        p, device = xy(k)
        sum_copy(p, device, True).wait_recv()
        return carry

    lax.fori_loop(1, GROUP, sum_wait, 0)
    numer = jnp.sum(boxes[1].astype(F32), axis=0)
    target_out[:, :128] = (numer[:, :128] / mass).astype(BF16)
    target_out[:, 128:] = (numer[:, 128:] / mass).astype(BF16)

    for k in range(1, NX):
        quarter(k)[1].wait_send()

    def drain(k, carry):
        p, device = xy(k)
        noise_copy(k, False).wait_send()
        sum_copy(p, device, False).wait_send()
        for turn in range(ITERS + 1):
            row_copy(turn, k, False).wait_send()
        for turn in range(ITERS):
            col_copy(turn, k, False).wait_send()
        return carry

    lax.fori_loop(1, GROUP, drain, 0)

    def drain_z(d, carry):
        piece_copy(d, False).wait_send()
        row_pot_copy(d, False).wait_send()
        return carry

    lax.fori_loop(1, NZ, drain_z, 0)

    def drain_core(d, carry):
        core_copy(d, False).wait_send()
        return carry

    lax.fori_loop(0, NZ, drain_core, 0)

    def drain_x(d, carry):
        col_pot_copy(d, False).wait_send()
        return carry

    lax.fori_loop(1, NX, drain_x, 0)


def shards(noise_latents, teacher_latent_rows):
    vmem = pl.BlockSpec(memory_space=pltpu.VMEM)
    dma = pltpu.SemaphoreType.DMA
    row_pot, col_pot, targets = pl.pallas_call(
        kernel,
        out_shape=(
            jax.ShapeDtypeStruct((16, 128), F32),
            jax.ShapeDtypeStruct((8, 128), F32),
            jax.ShapeDtypeStruct((SHARE, WIDTH), BF16),
        ),
        in_specs=[vmem, vmem],
        out_specs=(vmem, vmem, vmem),
        scratch_shapes=[
            pltpu.VMEM((NX, 32, PIECE), BF16),
            pltpu.VMEM((NZ, NX, NC, 32, PIECE), BF16),
            pltpu.VMEM((GROUP, SHARE, WIDTH), BF16),
            pltpu.VMEM((NZ * PIECE, WIDTH), BF16),
            pltpu.VMEM((NZ, BLOCK_ROWS, PIECE), F32),
            pltpu.VMEM((BLOCK_ROWS, 128), F32),
            pltpu.VMEM((BLOCK_ROWS, 128), F32),
            pltpu.VMEM((CUTS, TILES, 128), F32),
            pltpu.VMEM((CUTS, TILES, 128), F32),
            pltpu.VMEM((2 * CUT, NZ * PIECE), BF16),
            pltpu.VMEM((ITERS + 1, GROUP, 8, 128), F32),
            pltpu.VMEM((ITERS, GROUP, TILES, 128), F32),
            pltpu.VMEM((NZ, 8, 128), F32),
            pltpu.VMEM((NX, TILES, 128), F32),
            pltpu.VMEM((4, 8, 128), F32),
            pltpu.VMEM((2, GROUP, SHARE, WIDTH), BF16),
            dma((NX,)), dma((NX,)),
            dma((GROUP,)), dma((GROUP,)),
            dma((NZ,)), dma((NZ,)),
            dma((NZ,)), dma((NZ,)),
            dma((ITERS + 1, GROUP)), dma((ITERS + 1, GROUP)),
            dma((ITERS, GROUP)), dma((ITERS, GROUP)),
            dma((GROUP,)), dma((GROUP,)),
            dma((NZ,)), dma((NZ,)),
            dma((NX,)), dma((NX,)),
        ],
        compiler_params=pltpu.CompilerParams(
            collective_id=0, has_side_effects=True, vmem_limit_bytes=48 * 2**20),
        name="sinkhorn",
    )(noise_latents, teacher_latent_rows)
    return row_pot.reshape(2048), col_pot.reshape(1024), targets


def solution(mesh):
    return jax.shard_map(
        shards,
        mesh=mesh,
        in_specs=(P(("noise", "sample"), None), P("sample", "noise")),
        out_specs=(P("noise"), P("sample"), P(("noise", "sample"), None)),
        check_vma=False,
    )
```

time: 812 us -> 89.3 us (0.11)
  blocking collectives: 585 us -> 0 us
  waiting for transfers between devices: 142 us -> 0 us
  Pallas kernels: 0 us -> 85.7 us
  other arithmetic: 54.1 us -> 0 us
  between operations: 14.2 us -> 0.66 us
  matrix products: 12 us -> 0 us
    pmax x6 -> x0, blocking collectives: 302 us -> none  [the longest x3 176 us: source_logsumexp_partial(): peak = lax.pmax(local_peak, 'sample')]
    psum x7 -> x0, blocking collectives: 267 us -> none  [the longest x3 171 us: source_logsumexp_partial(): total = lax.psum(jnp.sum(jnp.exp(scores - peak[:, None]), axis=1), 'sample')]
    pallas_call x0 -> x1, Pallas kernels: none -> 85.7 us  [shards(): pl.pallas_call(kernel, out_shape=(jax.ShapeDtypeStruct((16, 128), F32), j...]
    psum x1 -> x0, waiting for transfers between devices: 80 us -> none  [shards(): numer_all, mass_all = lax.psum((numer, mass_part), 'sample')]
    all_gather x1 -> x0, waiting for transfers between devices: 61.7 us -> none  [shards(): rows_x = lax.all_gather(noise_latents, 'sample', axis=0, tiled=True)]
    reduce_sum x9 -> x0, other arithmetic: 32.5 us -> none  [the longest x3 13.4 us: source_logsumexp_partial(): total = lax.psum(jnp.sum(jnp.exp(scores - peak[:, None]), axis=1), 'sample')]
    reduce_max x5 -> x0, other arithmetic: 20 us -> none  [the longest x3 12 us: col_lse(): local_peak = jnp.max(scores, axis=0)]
    all_gather x1 -> x0, blocking collectives: 16.4 us -> none  [shards(): cols_y = lax.all_gather(teacher_latent_rows, 'noise', axis=1, tiled=True)]
  transfers between devices with their start and end apart: 2 -> 0, of which waited for: 2 -> 0; matrix products, arithmetic and copies ran while one was open for 1% -> 0% of each run, Pallas kernels for 0% -> 0%
where the time goes in v1:
time: 89.3 us; the launch traced here: 89.2 us
  Pallas kernels  85.7 us (96%)
  local copies, waits for them, and re-layouts  2.82 us (3%)
    pallas_call x1, Pallas kernels, shards(): pl.pallas_call(kernel, out_shape=(jax.ShapeDtypeStruct((16, 128), F32), j...  85.7 us
    unnamed x6, local copies, waits for them, and re-layouts  2.82 us

profile of v1, /device:TPU:1, one launch (start us, length us, event | category | flops | bytes accessed | tf_op | source)
XLA Modules:
  0.0 89.2 jit_solution(7928196279716935876)
XLA Ops:
  0.6 0.0 copy-start
  0.6 1.0 %copy.5.teach_ref = bf16[1024,32]{1,0:T(8,128)(2,1)S(1)} copy(bf16[1024,32]{0,1:T(8,128)(2,1)} %param.3) | data formatting | bytes 131072 | tf_op args[1]
  1.7 0.0 copy-done
  1.7 85.7 %sinkhorn.1 = (f32[16,128]{1,0:T(8,128)S(1)}, f32[8,128]{1,0:T(8,128)S(1)}, bf16[64,256]{1,0:T(8,128)(2,1)S(1)}) custom-call(bf16[64,256]{1,0:T(8,128)(2,1)S(1)} %copy-done, bf16[1024,32]{1,0:T(8,128)(2,1)S(1)} %copy.5.teach_ref), custom_call_target="tpu_custom_call" | custom-call | tf_op jit(solution)/shard_map/sinkhorn/pallas_call | solution.py:434
  87.4 0.6 copy.9
  88.0 0.6 copy.10
  88.6 0.6 copy.11
Async XLA Ops:
  0.6 1.0 %copy-start = (bf16[64,256]{1,0:T(8,128)(2,1)S(1)}, bf16[64,256]{1,0:T(8,128)(2,1)}, u32[]{:S(2)}) copy-start(bf16[64,256]{1,0:T(8,128)(2,1)} %noise_ref.1) | copy-start | bytes 98308

commit v2 on v0

v2 whole, which is shorter than its diff:
```python
import math

import jax
import jax.numpy as jnp
from jax import lax
from jax.experimental import pallas as pl
from jax.experimental.pallas import tpu as pltpu
from jax.sharding import PartitionSpec as P

ITERS = 3
WIDTH = 256
ROWS, COLS = 16384, 32768
STRENGTH = 0.1
NX, NY, NZ, NC = 4, 4, 8, 2
GROUP = NX * NY
SHARE = 64
BLOCK_ROWS = GROUP * SHARE
PIECE = 256
CUT = 128
CUTS = BLOCK_ROWS // CUT
TILES = NZ * PIECE // 128
MESH = pl.DeviceIdType.MESH
F32, BF16 = jnp.float32, jnp.bfloat16
LN2 = math.log(2.0)
COST = 1.0 / (WIDTH * STRENGTH)


def spread(row):
    return jnp.broadcast_to(row, (128, 128)).T


def log2(a):
    return jnp.log(a) * (1.0 / LN2)


def lanes_of(t):
    return slice((t % 2) * 128, (t % 2) * 128 + 128)


def kernel(noise_hbm, teach_hbm, row_out, col_out, target_out, slices, cols, rows_x, tall, score, peak, total,
           gain, beta, plan, row_box, col_box, core_box, row_pot, col_pot, mine, mass_box, boxes,
           load, sa, ra, sx, rx, sz, rz, sc, rc, srow, rrow, scol, rcol, score_s, score_r, sm, rm, sn, rn, so, ro, sp, rp):
    n, s = lax.axis_index("noise"), lax.axis_index("sample")
    x, c = lax.div(n, NC), lax.rem(n, NC)
    y, z = lax.div(s, NZ), lax.rem(s, NZ)
    me = x * NY + y
    other = 1 - c
    xs = [x] + [lax.rem(x + d, NX) for d in range(1, NX)]
    ys = [y] + [lax.rem(y + d, NY) for d in range(1, NY)]
    zs = [z] + [lax.rem(z + d, NZ) for d in range(1, NZ)]
    noise_at = [px * NC + c for px in xs]
    across = [py * NZ + z for py in ys]
    along = [y * NZ + pz for pz in zs]
    sibling = (x * NC + other, s)
    near = [1, 7, 2, 6, 3, 5, 4]
    xy = [(noise_at[k // NY], across[k % NY]) for k in range(1, GROUP)]

    def send(src, dst, send_sem, recv_sem, device):
        pltpu.make_async_remote_copy(src_ref=src, dst_ref=dst, send_sem=send_sem, recv_sem=recv_sem,
                                     device_id=device, device_id_type=MESH).start()

    def wait(ref, sem):
        pltpu.make_async_copy(ref, ref, sem).wait()

    loads = [pltpu.make_async_copy(teach_hbm.at[:, q * PIECE:(q + 1) * PIECE], slices.at[q], load.at[q])
             for q in range(NX)]
    loads.append(pltpu.make_async_copy(noise_hbm, rows_x.at[me], load.at[NX]))
    for copy in loads:
        copy.start()

    barrier = pltpu.get_barrier_semaphore()
    greeted = xy + [(n, along[d]) for d in range(1, NZ)] + [sibling]
    for device in greeted:
        pl.semaphore_signal(barrier, inc=1, device_id=device, device_id_type=MESH)
    peak[...] = jnp.full((BLOCK_ROWS, 128), -1e30, F32)
    total[...] = jnp.zeros((BLOCK_ROWS, 128), F32)
    for copy in loads:
        copy.wait()
    cols[z, x, c] = slices[x]
    pl.semaphore_wait(barrier, len(greeted))

    for d in range(1, NX):
        send(slices.at[xs[d]], cols.at[z, x, c], sa.at[0], ra.at[0], (noise_at[d], s))
    for device in xy:
        send(rows_x.at[me], rows_x.at[me], sx.at[0], rx.at[0], device)
    wait(slices.at[0:NX - 1], ra.at[0])

    for d in near:
        send(cols.at[z, :, c], cols.at[z, :, c], sz.at[0], rz.at[z], (n, along[d]))
    send(cols.at[z, :, c], cols.at[z, :, c], sc.at[0], rc.at[z], sibling)
    wait(rows_x.at[0:GROUP - 1], rx.at[0])

    def scores_of(pz):
        block = cols[pz].reshape(WIDTH, PIECE)
        wide = block.astype(F32)
        norms = jnp.sum(wide * wide, axis=0, keepdims=True) * (COST / LN2)
        for b in range(CUTS):
            r = slice(b * CUT, (b + 1) * CUT)
            latents = rows_x[2 * b:2 * b + 2].reshape(CUT, WIDTH)
            dots = jnp.dot(latents, block, preferred_element_type=F32)
            h = dots * (2.0 * COST / LN2) - norms
            score[pz, r, :] = h
            left, right = h[:, :128], h[:, 128:]
            old = peak[r, :]
            new = jnp.maximum(old, jnp.maximum(left, right))
            total[r, :] = total[r, :] * jnp.exp2(old - new) + (jnp.exp2(left - new) + jnp.exp2(right - new))
            peak[r, :] = new

    def away(k):
        return lax.div(k + 1, 2) * (2 * lax.rem(k, 2) - 1) + NZ

    def piece(k, carry):
        @pl.when(k < NZ)
        def _():
            pz = lax.rem(z + away(k), NZ)
            wait(cols.at[pz, :, c], rz.at[pz])
            send(cols.at[pz, :, c], cols.at[pz, :, c], sc.at[0], rc.at[pz], sibling)

        pz = lax.rem(z + away(k - 1), NZ)
        wait(cols.at[pz, :, other], rc.at[pz])
        scores_of(pz)
        return carry

    lax.fori_loop(1, NZ + 1, piece, 0)

    def row_start(turn):
        for device in xy:
            send(row_box.at[turn, me], row_box.at[turn, me], srow.at[turn], rrow.at[turn], device)

    def row_wait(turn):
        wait(row_box.at[turn, 0:GROUP - 1], rrow.at[turn])

    def col_start(turn):
        for d in near:
            send(col_box.at[turn, z], col_box.at[turn, z], scol.at[turn], rcol.at[turn], (n, along[d]))

    def col_wait(turn):
        wait(col_box.at[turn, 0:NZ - 1], rcol.at[turn])

    def core_trade(turn, value):
        core_box[turn, c] = value
        send(core_box.at[turn, c], core_box.at[turn, c], score_s.at[turn], score_r.at[turn], sibling)
        wait(core_box.at[turn, other], score_r.at[turn])
        return core_box[turn]

    def log_sum(logs):
        top = jnp.max(logs, axis=0)
        return top + log2(jnp.sum(jnp.exp2(logs - top), axis=0))

    for b in range(CUTS):
        r = slice(b * CUT, (b + 1) * CUT)
        lane_peak = peak[r, :].T
        lane_total = total[r, :].T
        top = jnp.max(lane_peak, axis=0, keepdims=True)
        sums = jnp.sum(lane_total * jnp.exp2(lane_peak - top), axis=0, keepdims=True)
        row_box[0, me, b:b + 1, :] = top + log2(sums)
    row_start(0)
    for pz in range(NZ):
        block = cols[pz].reshape(WIDTH, PIECE).astype(F32)
        tall[pz * PIECE:(pz + 1) * PIECE, :] = block.T.astype(BF16)
    for b in range(CUTS):
        latents = rows_x[2 * b:2 * b + 2].reshape(CUT, WIDTH).astype(F32)
        squares = latents * latents
        mine[0, b:b + 1, :] = jnp.sum((squares[:, :128] + squares[:, 128:]).T, axis=0, keepdims=True)
    row_wait(0)
    row_log = -math.log2(ROWS) - log_sum(row_box[0])

    mine[1] = row_log

    def first_column(b, carry):
        r = pl.ds(pl.multiple_of(b * CUT, CUT), CUT)
        shift = spread(mine[1, pl.ds(b, 1), :])
        for t in range(TILES):
            h = (score[t // 2, r, lanes_of(t)] + shift).reshape(CUT // 8, 8, 128)
            top = jnp.max(h, axis=0)
            e = jnp.exp2(h - top)
            score[t // 2, r, lanes_of(t)] = e.reshape(CUT, 128)
            gain[b, t] = top
            beta[b, t] = jnp.sum(e, axis=0)
        return carry

    lax.fori_loop(0, CUTS, first_column, 0)
    for t in range(TILES):
        cut_peak = gain[:, t]
        top = jnp.max(jnp.max(cut_peak, axis=0), axis=0, keepdims=True)
        sums = jnp.sum(jnp.sum(beta[:, t] * jnp.exp2(cut_peak - top), axis=0), axis=0, keepdims=True)
        col_box[0, z, t:t + 1, :] = top + log2(sums)
    col_start(0)
    col_wait(0)
    col_log = -math.log2(COLS) - log_sum(core_trade(0, log_sum(col_box[0])))
    for t in range(TILES):
        start_gain = jnp.exp2(gain[:, t] + col_log[t:t + 1, :])
        gain[:, t] = start_gain
        beta[:, t] = start_gain

    alpha = None
    for turn in range(1, ITERS):
        for b in range(CUTS):
            r = slice(b * CUT, (b + 1) * CUT)
            acc = None
            for t in range(TILES):
                term = score[t // 2, r, lanes_of(t)].reshape(CUT // 8, 8, 128) * beta[b, t]
                acc = term if acc is None else acc + term
            row_box[turn, me, b:b + 1, :] = jnp.sum(acc.reshape(CUT, 128).T, axis=0, keepdims=True)
        row_start(turn)
        row_wait(turn)
        alpha = 1.0 / (ROWS * jnp.sum(row_box[turn], axis=0))
        mine[2] = alpha

        sums = [None] * TILES
        for b in range(CUTS):
            r = slice(b * CUT, (b + 1) * CUT)
            weight = spread(alpha[b:b + 1, :])
            for t in range(TILES):
                term = score[t // 2, r, lanes_of(t)] * weight
                term = jnp.sum(term.reshape(CUT // 8, 8, 128), axis=0) * gain[b, t]
                sums[t] = term if b == 0 else sums[t] + term
        for t in range(TILES):
            col_box[turn, z, t:t + 1, :] = jnp.sum(sums[t], axis=0, keepdims=True)
        col_start(turn)
        col_wait(turn)
        pair = core_trade(turn, jnp.sum(col_box[turn], axis=0))
        factor = 1.0 / (COLS * (pair[0] + pair[1]))
        for t in range(TILES):
            beta[:, t] = gain[:, t] * factor[t:t + 1, :]

    row_pot[z] = COST * mine[0] + LN2 * (row_log + log2(alpha))
    col_pot[x] = LN2 * (col_log + log2(factor))
    for d in near:
        send(row_pot.at[z], row_pot.at[z], so.at[0], ro.at[0], (n, along[d]))
    for d in range(1, NX):
        send(col_pot.at[x], col_pot.at[x], sp.at[0], rp.at[0], (noise_at[d], s))

    def project(px, peers):
        for half in range(2):
            b = px * 2 + half
            r = pl.ds(pl.multiple_of(b * CUT, CUT), CUT)
            weight = spread(mine[2, pl.ds(b, 1), :])
            acc = None
            for t in range(TILES):
                p = (score[t // 2, r, lanes_of(t)] * weight).reshape(CUT // 8, 8, 128) * beta[b, t]
                acc = p if acc is None else acc + p
                plan[half * CUT:half * CUT + CUT, t * 128:t * 128 + 128] = p.reshape(CUT, 128).astype(BF16)
            mass_box[0, px, half:half + 1, :] = jnp.sum(acc.reshape(CUT, 128).T, axis=0, keepdims=True)
        numer = jnp.dot(plan[...], tall[...], preferred_element_type=F32).astype(BF16)
        for py in range(NY):
            boxes[0, px * NY + py] = numer[py * SHARE:(py + 1) * SHARE, :]
        for d, device in peers:
            send(mass_box.at[0, px], mass_box.at[1, me], sm.at[0], rm.at[0], device)
            send(boxes.at[0, px * NY + ys[d]], boxes.at[1, me], sn.at[0], rn.at[0], device)

    for k in range(1, NX):
        project(xs[k], [(d, (noise_at[k], across[d])) for d in range(NY)])
    project(x, [(d, (n, across[d])) for d in range(1, NY)])
    boxes[1, me] = boxes[0, me]
    mass_box[1, me] = mass_box[0, x]

    wait(col_pot.at[0:NX - 1], rp.at[0])
    for px in range(NX):
        for half in range(2):
            col_out[2 * px + half:2 * px + half + 1, :] = col_pot[px, pl.ds(2 * z + half, 1), :]
    wait(row_pot.at[0:NZ - 1], ro.at[0])
    low = lax.broadcasted_iota(jnp.int32, (1, 128), 1) < SHARE
    for py in range(NY):
        for pair in range(NZ // 2):
            even = row_pot[2 * pair, pl.ds(2 * x + py // 2, 1), :]
            odd = row_pot[2 * pair + 1, pl.ds(2 * x + py // 2, 1), :]
            if py % 2:
                even = pltpu.roll(even, SHARE, 1)
            else:
                odd = pltpu.roll(odd, SHARE, 1)
            row_out[4 * py + pair:4 * py + pair + 1, :] = jnp.where(low, even, odd)

    wait(mass_box.at[1, 0:GROUP - 1], rm.at[0])
    mine[3] = jnp.sum(mass_box[1], axis=0)
    total[0:128, :] = spread(mine[3, pl.ds(lax.div(y, 2), 1), :])
    mass = total[pl.ds(pl.multiple_of(lax.rem(y, 2) * SHARE, SHARE), SHARE), :]
    wait(boxes.at[1, 0:GROUP - 1], rn.at[0])
    numer = jnp.sum(boxes[1].astype(F32), axis=0)
    target_out[:, :128] = (numer[:, :128] / mass).astype(BF16)
    target_out[:, 128:] = (numer[:, 128:] / mass).astype(BF16)

    wait(slices.at[0:NX - 1], sa.at[0])
    wait(rows_x.at[0:GROUP - 1], sx.at[0])
    wait(cols.at[0:NZ - 1, :, c], sz.at[0])
    wait(cols.at[:, :, c], sc.at[0])
    for turn in range(ITERS):
        wait(row_box.at[turn, 0:GROUP - 1], srow.at[turn])
        wait(col_box.at[turn, 0:NZ - 1], scol.at[turn])
        wait(core_box.at[turn, c], score_s.at[turn])
    wait(row_pot.at[0:NZ - 1], so.at[0])
    wait(col_pot.at[0:NX - 1], sp.at[0])
    wait(mass_box.at[1, 0:GROUP - 1], sm.at[0])
    wait(boxes.at[1, 0:GROUP - 1], sn.at[0])


def give(a, b, c, a_out, b_out, c_out, sems):
    copies = [pltpu.make_async_copy(src, dst, sems.at[k])
              for k, (src, dst) in enumerate(((a, a_out), (b, b_out), (c, c_out)))]
    for copy in copies:
        copy.start()
    for copy in copies:
        copy.wait()


def shards(noise_latents, teacher_latent_rows):
    vmem = pl.BlockSpec(memory_space=pltpu.VMEM)
    hbm = pl.BlockSpec(memory_space=pltpu.HBM)
    dma = pltpu.SemaphoreType.DMA
    shapes = (
        jax.ShapeDtypeStruct((16, 128), F32),
        jax.ShapeDtypeStruct((8, 128), F32),
        jax.ShapeDtypeStruct((SHARE, WIDTH), BF16),
    )
    results = pl.pallas_call(
        kernel,
        out_shape=shapes,
        in_specs=[hbm, hbm],
        out_specs=(vmem, vmem, vmem),
        scratch_shapes=[
            pltpu.VMEM((NX, 32, PIECE), BF16),
            pltpu.VMEM((NZ, NX, NC, 32, PIECE), BF16),
            pltpu.VMEM((GROUP, SHARE, WIDTH), BF16),
            pltpu.VMEM((NZ * PIECE, WIDTH), BF16),
            pltpu.VMEM((NZ, BLOCK_ROWS, PIECE), F32),
            pltpu.VMEM((BLOCK_ROWS, 128), F32),
            pltpu.VMEM((BLOCK_ROWS, 128), F32),
            pltpu.VMEM((CUTS, TILES, 8, 128), F32),
            pltpu.VMEM((CUTS, TILES, 8, 128), F32),
            pltpu.VMEM((2 * CUT, NZ * PIECE), BF16),
            pltpu.VMEM((ITERS, GROUP, 8, 128), F32),
            pltpu.VMEM((ITERS, NZ, TILES, 128), F32),
            pltpu.VMEM((ITERS, NC, TILES, 128), F32),
            pltpu.VMEM((NZ, 8, 128), F32),
            pltpu.VMEM((NX, TILES, 128), F32),
            pltpu.VMEM((4, 8, 128), F32),
            pltpu.VMEM((2, GROUP, 8, 128), F32),
            pltpu.VMEM((2, GROUP, SHARE, WIDTH), BF16),
            dma((NX + 1,)),
            dma((1,)), dma((1,)),
            dma((1,)), dma((1,)),
            dma((1,)), dma((NZ,)),
            dma((1,)), dma((NZ,)),
            dma((ITERS,)), dma((ITERS,)),
            dma((ITERS,)), dma((ITERS,)),
            dma((ITERS,)), dma((ITERS,)),
            dma((1,)), dma((1,)),
            dma((1,)), dma((1,)),
            dma((1,)), dma((1,)),
            dma((1,)), dma((1,)),
        ],
        compiler_params=pltpu.CompilerParams(
            collective_id=0, has_side_effects=True, vmem_limit_bytes=55172 * 1024),
        name="sinkhorn",
    )(noise_latents, teacher_latent_rows.T)
    row_pot, col_pot, targets = pl.pallas_call(
        give,
        out_shape=shapes,
        in_specs=[vmem, vmem, vmem],
        out_specs=(hbm, hbm, hbm),
        scratch_shapes=[dma((3,))],
        compiler_params=pltpu.CompilerParams(vmem_limit_bytes=2**20),
        name="give",
    )(*results)
    return row_pot.reshape(2048), col_pot.reshape(1024), targets


def solution(mesh):
    return jax.shard_map(
        shards,
        mesh=mesh,
        in_specs=(P(("noise", "sample"), None), P("sample", "noise")),
        out_specs=(P("noise"), P("sample"), P(("noise", "sample"), None)),
        check_vma=False,
    )
```

time: 812 us -> 79.7 us (0.10)
  blocking collectives: 585 us -> 0 us
  waiting for transfers between devices: 142 us -> 0 us
  Pallas kernels: 0 us -> 78.9 us
  other arithmetic: 54.1 us -> 0 us
  between operations: 14.2 us -> 0.64 us
  matrix products: 12 us -> 0 us
    pmax x6 -> x0, blocking collectives: 302 us -> none  [the longest x3 176 us: source_logsumexp_partial(): peak = lax.pmax(local_peak, 'sample')]
    psum x7 -> x0, blocking collectives: 267 us -> none  [the longest x3 171 us: source_logsumexp_partial(): total = lax.psum(jnp.sum(jnp.exp(scores - peak[:, None]), axis=1), 'sample')]
    psum x1 -> x0, waiting for transfers between devices: 80 us -> none  [shards(): numer_all, mass_all = lax.psum((numer, mass_part), 'sample')]
    pallas_call x0 -> x2, Pallas kernels: none -> 78.9 us  [the longest x1 78.3 us: shards(): pl.pallas_call(kernel, out_shape=shapes, in_specs=[hbm, hbm], out_specs=(...]
    all_gather x1 -> x0, waiting for transfers between devices: 61.7 us -> none  [shards(): rows_x = lax.all_gather(noise_latents, 'sample', axis=0, tiled=True)]
    reduce_sum x9 -> x0, other arithmetic: 32.5 us -> none  [the longest x3 13.4 us: source_logsumexp_partial(): total = lax.psum(jnp.sum(jnp.exp(scores - peak[:, None]), axis=1), 'sample')]
    reduce_max x5 -> x0, other arithmetic: 20 us -> none  [the longest x3 12 us: col_lse(): local_peak = jnp.max(scores, axis=0)]
    all_gather x1 -> x0, blocking collectives: 16.4 us -> none  [shards(): cols_y = lax.all_gather(teacher_latent_rows, 'noise', axis=1, tiled=True)]
  transfers between devices with their start and end apart: 2 -> 0, of which waited for: 2 -> 0; matrix products, arithmetic and copies ran while one was open for 1% -> 0% of each run, Pallas kernels for 0% -> 0%
where the time goes in v2:
time: 79.7 us; the launch traced here: 79.6 us
  Pallas kernels  78.9 us (99%)
    pallas_call x1, Pallas kernels, shards(): pl.pallas_call(kernel, out_shape=shapes, in_specs=[hbm, hbm], out_specs=(...  78.3 us

profile of v2, /device:TPU:1, one launch (start us, length us, event | category | flops | bytes accessed | tf_op | source)
XLA Modules:
  0.0 79.6 jit_solution(3629988005313229490)
XLA Ops:
  0.6 78.3 %sinkhorn.1 = (f32[16,128]{1,0:T(8,128)S(1)}, f32[8,128]{1,0:T(8,128)S(1)}, bf16[64,256]{1,0:T(8,128)(2,1)S(1)}) custom-call(bf16[64,256]{1,0:T(8,128)(2,1)} %noise_hbm.1, bf16[32,1024]{1,0:T(8,128)(2,1)} %bitcast.3), custom_call_target="tpu_custom_call" | custom-call | tf_op jit(solution)/shard_map/sinkhorn/pallas_call | solution.py:315
  78.9 0.7 give.1

commit v3 on v2

v3 whole, which is shorter than its diff:
```python
import math

import jax
import jax.numpy as jnp
from jax import lax
from jax.experimental import pallas as pl
from jax.experimental.pallas import tpu as pltpu
from jax.sharding import PartitionSpec as P

ITERS = 3
WIDTH = 256
ROWS, COLS = 16384, 32768
STRENGTH = 0.1
NX, NY, NZ, NC = 4, 4, 8, 2
GROUP = NX * NY
SHARE = 64
BLOCK_ROWS = NZ * NC * SHARE
HALF = 512
FEATURES = WIDTH // (NX * NC)
PIECE = 256
PIECES = NY * HALF // PIECE
CUT = NC * SHARE
CUTS = NZ
TILES = PIECES * PIECE // 128
MESH = pl.DeviceIdType.MESH
F32, BF16 = jnp.float32, jnp.bfloat16
LN2 = math.log(2.0)
COST = 1.0 / (WIDTH * STRENGTH)


def spread(row):
    return jnp.broadcast_to(row, (128, 128)).T


def log2(a):
    return jnp.log(a) * (1.0 / LN2)


def lanes_of(t):
    return slice((t % 2) * 128, (t % 2) * 128 + 128)


def kernel(noise_hbm, teach_hbm, row_out, col_out, target_out, offer, cols, rows_x, tall, score, peak, total,
           gain, beta, plan, row_box, core_box, col_box, row_pot, col_pot, mine, gifts, boxes,
           load, s_offer, r_offer, s_x, s_y, r_x, r_y, s_xy, s_yx, r_xy, r_yx, s_rows, r_rows, s_pair, r_pair,
           s_row, r_row, s_core, r_core, s_col, r_col, s_rpot, r_rpot, s_cpot, r_cpot, s_gift, r_gift, s_box, r_box):
    n, s = lax.axis_index("noise"), lax.axis_index("sample")
    x, c = lax.div(n, NC), lax.rem(n, NC)
    y, z = lax.div(s, NZ), lax.rem(s, NZ)
    me = x * NY + y
    other = 1 - c
    xs = [x] + [lax.rem(x + d, NX) for d in range(1, NX)]
    ys = [y] + [lax.rem(y + d, NY) for d in range(1, NY)]
    zs = [z] + [lax.rem(z + d, NZ) for d in range(1, NZ)]
    noise_at = [px * NC + c for px in xs]
    across = [py * NZ + z for py in ys]
    along = [y * NZ + pz for pz in zs]
    sibling = (x * NC + other, s)
    xy = [(noise_at[k // NY], across[k % NY]) for k in range(1, GROUP)]
    ring = [1, 3, 2]
    near = [1, 7, 2, 6, 3, 5, 4]

    def send(src, dst, send_sem, recv_sem, device):
        pltpu.make_async_remote_copy(src_ref=src, dst_ref=dst, send_sem=send_sem, recv_sem=recv_sem,
                                     device_id=device, device_id_type=MESH).start()

    def wait(ref, sem):
        pltpu.make_async_copy(ref, ref, sem).wait()

    def half(which):
        return teach_hbm.at[:, pl.ds(pl.multiple_of(which * HALF, HALF), HALF)]

    own = cols.at[y, x, c]
    theirs = cols.at[y, x, other]
    loads = [pltpu.make_async_copy(half(other), offer, load.at[0]),
             pltpu.make_async_copy(half(c), own, load.at[1]),
             pltpu.make_async_copy(noise_hbm, rows_x.at[z, c], load.at[2])]
    for copy in loads:
        copy.start()

    barrier = pltpu.get_barrier_semaphore()
    greeted = xy + [(n, along[d]) for d in range(1, NZ)] + [sibling]
    for device in greeted:
        pl.semaphore_signal(barrier, inc=1, device_id=device, device_id_type=MESH)
    peak[...] = jnp.full((BLOCK_ROWS, 128), -1e30, F32)
    total[...] = jnp.zeros((BLOCK_ROWS, 128), F32)
    for copy in loads:
        copy.wait()
    pl.semaphore_wait(barrier, len(greeted))

    send(offer, cols.at[y, x, c], s_offer.at[0], r_offer.at[0], sibling)
    for d in ring:
        send(own, own, s_x.at[0], r_x.at[x], (noise_at[d], s))
        send(own, own, s_x.at[0], r_xy.at[y], (n, across[d]))
    for d in near:
        send(rows_x.at[z, c], rows_x.at[z, c], s_rows.at[0], r_rows.at[z], (n, along[d]))
    send(rows_x.at[z, c], rows_x.at[z, c], s_pair.at[0], r_pair.at[0], sibling)
    wait(theirs, r_offer.at[0])
    for d in ring:
        send(theirs, theirs, s_y.at[0], r_y.at[y], (n, across[d]))
        send(theirs, theirs, s_y.at[0], r_yx.at[y], (noise_at[d], s))
    for d in ring:
        passed = cols.at[y, xs[d], c]
        wait(passed, r_x.at[xs[d]])
        for e in ring:
            send(passed, passed, s_xy.at[0], r_xy.at[y], (n, across[e]))
        passed = cols.at[ys[d], x, other]
        wait(passed, r_y.at[ys[d]])
        for e in ring:
            send(passed, passed, s_yx.at[0], r_yx.at[ys[d]], (noise_at[e], s))
    for d in near:
        passed = rows_x.at[zs[d], c]
        wait(passed, r_rows.at[zs[d]])
        send(passed, passed, s_pair.at[0], r_pair.at[0], sibling)
    wait(rows_x.at[:, other], r_pair.at[0])

    def block_of(py, part):
        return cols[py, :, :, :, part * PIECE:(part + 1) * PIECE].reshape(WIDTH, PIECE)

    def scores_of(py, part):
        block = block_of(py, part)
        wide = block.astype(F32)
        norms = jnp.sum(wide * wide, axis=0, keepdims=True) * (COST / LN2)
        for b in range(CUTS):
            r = slice(b * CUT, (b + 1) * CUT)
            dots = jnp.dot(rows_x[b].reshape(CUT, WIDTH), block, preferred_element_type=F32)
            h = dots * (2.0 * COST / LN2) - norms
            score[py * 2 + part, r, :] = h
            left, right = h[:, :128], h[:, 128:]
            old = peak[r, :]
            new = jnp.maximum(old, jnp.maximum(left, right))
            total[r, :] = total[r, :] * jnp.exp2(old - new) + (jnp.exp2(left - new) + jnp.exp2(right - new))
            peak[r, :] = new

    def piece(k, carry):
        py = lax.rem(y + k, NY)

        @pl.when(k > 0)
        def _():
            wait(cols.at[py, :, c], r_xy.at[py])

        wait(cols.at[py, 0:NX - 1, other], r_yx.at[py])
        scores_of(py, 0)
        scores_of(py, 1)
        return carry

    lax.fori_loop(0, NY, piece, 0)

    def row_start(turn):
        for d in near:
            send(row_box.at[turn, z], row_box.at[turn, z], s_row.at[turn], r_row.at[turn], (n, along[d]))

    def row_wait(turn):
        wait(row_box.at[turn, 0:NZ - 1], r_row.at[turn])

    def core_trade(turn, value):
        core_box[turn, c] = value
        send(core_box.at[turn, c], core_box.at[turn, c], s_core.at[turn], r_core.at[turn], sibling)
        wait(core_box.at[turn, other], r_core.at[turn])
        return core_box[turn]

    def col_trade(turn):
        for device in xy:
            send(col_box.at[turn, me], col_box.at[turn, me], s_col.at[turn], r_col.at[turn], device)
        wait(col_box.at[turn, 0:GROUP - 1], r_col.at[turn])

    def log_sum(logs):
        top = jnp.max(logs, axis=0)
        return top + log2(jnp.sum(jnp.exp2(logs - top), axis=0))

    for b in range(CUTS):
        r = slice(b * CUT, (b + 1) * CUT)
        lane_peak = peak[r, :].T
        lane_total = total[r, :].T
        top = jnp.max(lane_peak, axis=0, keepdims=True)
        sums = jnp.sum(lane_total * jnp.exp2(lane_peak - top), axis=0, keepdims=True)
        row_box[0, z, b:b + 1, :] = top + log2(sums)
    row_start(0)
    for u in range(PIECES):
        tall[u * PIECE:(u + 1) * PIECE, :] = block_of(u // 2, u % 2).astype(F32).T.astype(BF16)
    for b in range(CUTS):
        latents = rows_x[b].reshape(CUT, WIDTH).astype(F32)
        squares = latents * latents
        mine[0, b:b + 1, :] = jnp.sum((squares[:, :128] + squares[:, 128:]).T, axis=0, keepdims=True)
    row_wait(0)
    row_log = -math.log2(ROWS) - log_sum(core_trade(0, log_sum(row_box[0])))

    mine[1] = row_log

    def first_column(b, carry):
        r = pl.ds(pl.multiple_of(b * CUT, CUT), CUT)
        shift = spread(mine[1, pl.ds(b, 1), :])
        for t in range(TILES):
            h = (score[t // 2, r, lanes_of(t)] + shift).reshape(CUT // 8, 8, 128)
            top = jnp.max(h, axis=0)
            e = jnp.exp2(h - top)
            score[t // 2, r, lanes_of(t)] = e.reshape(CUT, 128)
            gain[b, t] = top
            beta[b, t] = jnp.sum(e, axis=0)
        return carry

    lax.fori_loop(0, CUTS, first_column, 0)
    for t in range(TILES):
        cut_peak = gain[:, t]
        top = jnp.max(jnp.max(cut_peak, axis=0), axis=0, keepdims=True)
        sums = jnp.sum(jnp.sum(beta[:, t] * jnp.exp2(cut_peak - top), axis=0), axis=0, keepdims=True)
        col_box[0, me, t:t + 1, :] = top + log2(sums)
    col_trade(0)
    col_log = -math.log2(COLS) - log_sum(col_box[0])
    for t in range(TILES):
        start_gain = jnp.exp2(gain[:, t] + col_log[t:t + 1, :])
        gain[:, t] = start_gain
        beta[:, t] = start_gain

    alpha = None
    for turn in range(1, ITERS):
        for b in range(CUTS):
            r = slice(b * CUT, (b + 1) * CUT)
            acc = None
            for t in range(TILES):
                term = score[t // 2, r, lanes_of(t)].reshape(CUT // 8, 8, 128) * beta[b, t]
                acc = term if acc is None else acc + term
            row_box[turn, z, b:b + 1, :] = jnp.sum(acc.reshape(CUT, 128).T, axis=0, keepdims=True)
        row_start(turn)
        row_wait(turn)
        pair = core_trade(turn, jnp.sum(row_box[turn], axis=0))
        alpha = 1.0 / (ROWS * (pair[0] + pair[1]))

        sums = [None] * TILES
        for b in range(CUTS):
            r = slice(b * CUT, (b + 1) * CUT)
            weight = spread(alpha[b:b + 1, :])
            if turn == ITERS - 1:
                total[r, :] = weight
            for t in range(TILES):
                term = score[t // 2, r, lanes_of(t)] * weight
                term = jnp.sum(term.reshape(CUT // 8, 8, 128), axis=0) * gain[b, t]
                sums[t] = term if b == 0 else sums[t] + term
        for t in range(TILES):
            col_box[turn, me, t:t + 1, :] = jnp.sum(sums[t], axis=0, keepdims=True)
        col_trade(turn)
        factor = 1.0 / (COLS * jnp.sum(col_box[turn], axis=0))
        for t in range(TILES):
            beta[:, t] = gain[:, t] * factor[t:t + 1, :]

    order = [4, 3, 5, 2, 6, 7, 1, 0]

    def project(which, group):
        for k in range(4):
            pz = zs[order[4 * group + k]]
            r = pl.ds(pl.multiple_of(pz * CUT + which * SHARE, SHARE), SHARE)
            weight = total[r, :]
            acc = None
            for t in range(TILES):
                p = (score[t // 2, r, lanes_of(t)] * weight).reshape(SHARE // 8, 8, 128) * beta[pz, t]
                acc = p if acc is None else acc + p
                plan[k * SHARE:(k + 1) * SHARE, t * 128:t * 128 + 128] = p.reshape(SHARE, 128).astype(BF16)
            peak[r, :] = acc.reshape(SHARE, 128)
        return jnp.dot(plan[...], tall[...], preferred_element_type=F32)

    for group in range(2):
        gifts[0, group] = project(other, group).astype(BF16)
        send(gifts.at[0, group], gifts.at[1, group], s_gift.at[group], r_gift.at[group], sibling)
    for group in range(2):
        numer = project(c, group)
        wait(gifts.at[1, group], r_gift.at[group])
        numer = (numer + gifts[1, group].astype(F32)).astype(BF16)
        for k in range(4):
            d = order[4 * group + k]
            boxes[0, d] = numer[k * SHARE:(k + 1) * SHARE, :]
            if d:
                send(boxes.at[0, d], boxes.at[1, z], s_box.at[0], r_box.at[0], (n, along[d]))
    boxes[1, z] = boxes[0, 0]
    for b in range(CUTS):
        row_box[ITERS, z, b:b + 1, :] = jnp.sum(peak[b * CUT:(b + 1) * CUT, :].T, axis=0, keepdims=True)
    row_start(ITERS)

    row_pot[y] = COST * mine[0] + LN2 * (row_log + log2(alpha))
    col_pot[c] = LN2 * (col_log + log2(factor))
    for d in ring:
        send(row_pot.at[y], row_pot.at[y], s_rpot.at[0], r_rpot.at[0], (n, across[d]))
    send(col_pot.at[c], col_pot.at[c], s_cpot.at[0], r_cpot.at[0], sibling)
    wait(col_pot.at[other], r_cpot.at[0])
    for pc in range(NC):
        for q in range(HALF // 128):
            col_out[4 * pc + q:4 * pc + q + 1, :] = col_pot[pc, pl.ds(4 * y + q, 1), :]
    wait(row_pot.at[0:NY - 1], r_rpot.at[0])
    low = lax.broadcasted_iota(jnp.int32, (NZ // 2, 128), 1) < SHARE
    for py in range(NY):
        pairs = row_pot[py].reshape(NZ // 2, 2, 128)
        even, odd = pairs[:, 0], pairs[:, 1]
        even_low = jnp.where(c == 0, even, pltpu.roll(even, SHARE, 1))
        odd_high = jnp.where(c == 0, pltpu.roll(odd, SHARE, 1), odd)
        row_out[4 * py:4 * py + 4, :] = jnp.where(low, even_low, odd_high)

    row_wait(ITERS)
    pair = core_trade(ITERS, jnp.sum(row_box[ITERS], axis=0))
    mine[1] = pair[0] + pair[1]
    total[0:128, :] = spread(mine[1, pl.ds(z, 1), :])
    mass = total[pl.ds(pl.multiple_of(c * SHARE, SHARE), SHARE), :]
    wait(boxes.at[1, 0:NZ - 1], r_box.at[0])
    numer = jnp.sum(boxes[1].astype(F32), axis=0)
    target_out[:, :128] = (numer[:, :128] / mass).astype(BF16)
    target_out[:, 128:] = (numer[:, 128:] / mass).astype(BF16)

    wait(offer, s_offer.at[0])
    wait(cols.at[0, 0:3], s_x.at[0])
    wait(cols.at[0, 0:3], s_y.at[0])
    wait(cols.at[0:3, 0:3, 0], s_xy.at[0])
    wait(cols.at[0:3, 0:3, 0], s_yx.at[0])
    wait(rows_x.at[0:NZ - 1, 0], s_rows.at[0])
    wait(rows_x.at[:, 0], s_pair.at[0])
    for turn in range(ITERS + 1):
        wait(row_box.at[turn, 0:NZ - 1], s_row.at[turn])
        wait(core_box.at[turn, c], s_core.at[turn])
    for turn in range(ITERS):
        wait(col_box.at[turn, 0:GROUP - 1], s_col.at[turn])
    wait(row_pot.at[0:NY - 1], s_rpot.at[0])
    wait(col_pot.at[c], s_cpot.at[0])
    for group in range(2):
        wait(gifts.at[0, group], s_gift.at[group])
    wait(boxes.at[1, 0:NZ - 1], s_box.at[0])


def give(a, b, c, a_out, b_out, c_out, sems):
    copies = [pltpu.make_async_copy(src, dst, sems.at[k])
              for k, (src, dst) in enumerate(((a, a_out), (b, b_out), (c, c_out)))]
    for copy in copies:
        copy.start()
    for copy in copies:
        copy.wait()


def shards(noise_latents, teacher_latent_rows):
    vmem = pl.BlockSpec(memory_space=pltpu.VMEM)
    hbm = pl.BlockSpec(memory_space=pltpu.HBM)
    dma = pltpu.SemaphoreType.DMA
    shapes = (
        jax.ShapeDtypeStruct((16, 128), F32),
        jax.ShapeDtypeStruct((8, 128), F32),
        jax.ShapeDtypeStruct((SHARE, WIDTH), BF16),
    )
    results = pl.pallas_call(
        kernel,
        out_shape=shapes,
        in_specs=[hbm, hbm],
        out_specs=(vmem, vmem, vmem),
        scratch_shapes=[
            pltpu.VMEM((FEATURES, HALF), BF16),
            pltpu.VMEM((NY, NX, NC, FEATURES, HALF), BF16),
            pltpu.VMEM((NZ, NC, SHARE, WIDTH), BF16),
            pltpu.VMEM((PIECES * PIECE, WIDTH), BF16),
            pltpu.VMEM((PIECES, BLOCK_ROWS, PIECE), F32),
            pltpu.VMEM((BLOCK_ROWS, 128), F32),
            pltpu.VMEM((BLOCK_ROWS, 128), F32),
            pltpu.VMEM((CUTS, TILES, 8, 128), F32),
            pltpu.VMEM((CUTS, TILES, 8, 128), F32),
            pltpu.VMEM((4 * SHARE, PIECES * PIECE), BF16),
            pltpu.VMEM((ITERS + 1, NZ, 8, 128), F32),
            pltpu.VMEM((ITERS + 1, NC, 8, 128), F32),
            pltpu.VMEM((ITERS, GROUP, TILES, 128), F32),
            pltpu.VMEM((NY, 8, 128), F32),
            pltpu.VMEM((NC, TILES, 128), F32),
            pltpu.VMEM((2, 8, 128), F32),
            pltpu.VMEM((2, 2, 4 * SHARE, WIDTH), BF16),
            pltpu.VMEM((2, NZ, SHARE, WIDTH), BF16),
            dma((3,)),
            dma((1,)), dma((1,)),
            dma((1,)), dma((1,)), dma((NX,)), dma((NY,)),
            dma((1,)), dma((1,)), dma((NY,)), dma((NY,)),
            dma((1,)), dma((NZ,)),
            dma((1,)), dma((1,)),
            dma((ITERS + 1,)), dma((ITERS + 1,)),
            dma((ITERS + 1,)), dma((ITERS + 1,)),
            dma((ITERS,)), dma((ITERS,)),
            dma((1,)), dma((1,)),
            dma((1,)), dma((1,)),
            dma((2,)), dma((2,)),
            dma((1,)), dma((1,)),
        ],
        compiler_params=pltpu.CompilerParams(
            collective_id=0, has_side_effects=True, vmem_limit_bytes=55172 * 1024),
        name="sinkhorn",
    )(noise_latents, teacher_latent_rows.T)
    row_pot, col_pot, targets = pl.pallas_call(
        give,
        out_shape=shapes,
        in_specs=[vmem, vmem, vmem],
        out_specs=(hbm, hbm, hbm),
        scratch_shapes=[dma((3,))],
        compiler_params=pltpu.CompilerParams(vmem_limit_bytes=2**20),
        name="give",
    )(*results)
    return row_pot.reshape(2048), col_pot.reshape(1024), targets


def solution(mesh):
    return jax.shard_map(
        shards,
        mesh=mesh,
        in_specs=(P(("noise", "sample"), None), P("sample", "noise")),
        out_specs=(P("noise"), P("sample"), P(("noise", "sample"), None)),
        check_vma=False,
    )
```

time: 79.7 us -> 75.7 us (0.950)
  Pallas kernels: 78.9 us -> 74.9 us
    pallas_call x1, Pallas kernels: 78.3 us -> 74.2 us  [shards(): pl.pallas_call(kernel, out_shape=shapes, in_specs=[hbm, hbm], out_specs=(...]
where the time goes in v3:
time: 75.7 us; the launch traced here: 75.5 us
  Pallas kernels  74.9 us (99%)
    pallas_call x1, Pallas kernels, shards(): pl.pallas_call(kernel, out_shape=shapes, in_specs=[hbm, hbm], out_specs=(...  74.2 us

profile of v3, /device:TPU:1, one launch (start us, length us, event | category | flops | bytes accessed | tf_op | source)
XLA Modules:
  0.0 75.5 jit_solution(5962301820930530252)
XLA Ops:
  0.6 74.2 %sinkhorn.1 = (f32[16,128]{1,0:T(8,128)S(1)}, f32[8,128]{1,0:T(8,128)S(1)}, bf16[64,256]{1,0:T(8,128)(2,1)S(1)}) custom-call(bf16[64,256]{1,0:T(8,128)(2,1)} %noise_hbm.1, bf16[32,1024]{1,0:T(8,128)(2,1)} %bitcast.3), custom_call_target="tpu_custom_call" | custom-call | tf_op jit(solution)/shard_map/sinkhorn/pallas_call | solution.py:343
  74.8 0.7 give.1

commit v4 on v3

--- a/solution.py
+++ b/solution.py
@@ -41,7 +41,7 @@
 
 
 def kernel(noise_hbm, teach_hbm, row_out, col_out, target_out, offer, cols, rows_x, tall, score, peak, total,
-           gain, beta, plan, row_box, core_box, col_box, row_pot, col_pot, mine, gifts, boxes,
+           gain, beta, plan, row_box, core_box, col_box, sum_box, row_pot, col_pot, mine, gifts, boxes,
            load, s_offer, r_offer, s_x, s_y, r_x, r_y, s_xy, s_yx, r_xy, r_yx, s_rows, r_rows, s_pair, r_pair,
            s_row, r_row, s_core, r_core, s_col, r_col, s_rpot, r_rpot, s_cpot, r_cpot, s_gift, r_gift, s_box, r_box):
     n, s = lax.axis_index("noise"), lax.axis_index("sample")
@@ -100,14 +100,15 @@
         send(theirs, theirs, s_y.at[0], r_y.at[y], (n, across[d]))
         send(theirs, theirs, s_y.at[0], r_yx.at[y], (noise_at[d], s))
     for d in ring:
-        passed = cols.at[y, xs[d], c]
-        wait(passed, r_x.at[xs[d]])
+        wait(cols.at[y, xs[d], c], r_x.at[xs[d]])
+    for q in (3, 1, 2):
+        for d in ring:
+            passed = cols.at[y, xs[d], c]
+            send(passed, passed, s_xy.at[0], r_xy.at[y], (n, across[NY - q]))
+        passed = cols.at[ys[q], x, other]
+        wait(passed, r_y.at[ys[q]])
         for e in ring:
-            send(passed, passed, s_xy.at[0], r_xy.at[y], (n, across[e]))
-        passed = cols.at[ys[d], x, other]
-        wait(passed, r_y.at[ys[d]])
-        for e in ring:
-            send(passed, passed, s_yx.at[0], r_yx.at[ys[d]], (noise_at[e], s))
+            send(passed, passed, s_yx.at[0], r_yx.at[ys[q]], (noise_at[e], s))
     for d in near:
         passed = rows_x.at[zs[d], c]
         wait(passed, r_rows.at[zs[d]])
@@ -133,7 +134,7 @@
             peak[r, :] = new
 
     def piece(k, carry):
-        py = lax.rem(y + k, NY)
+        py = lax.rem(y + lax.div(3 * k * (k + 1), 2), NY)
 
         @pl.when(k > 0)
         def _():
@@ -160,9 +161,10 @@
         return core_box[turn]
 
     def col_trade(turn):
+        box = col_box if turn == 0 else sum_box.at[turn - 1]
         for device in xy:
-            send(col_box.at[turn, me], col_box.at[turn, me], s_col.at[turn], r_col.at[turn], device)
-        wait(col_box.at[turn, 0:GROUP - 1], r_col.at[turn])
+            send(box.at[me], box.at[me], s_col.at[turn], r_col.at[turn], device)
+        wait(box.at[0:GROUP - 1], r_col.at[turn])
 
     def log_sum(logs):
         top = jnp.max(logs, axis=0)
@@ -188,8 +190,8 @@
     mine[1] = row_log
 
     def first_column(b, carry):
-        r = pl.ds(pl.multiple_of(b * CUT, CUT), CUT)
-        shift = spread(mine[1, pl.ds(b, 1), :])
+        r = slice(b * CUT, (b + 1) * CUT)
+        shift = spread(row_log[b:b + 1, :])
         for t in range(TILES):
             h = (score[t // 2, r, lanes_of(t)] + shift).reshape(CUT // 8, 8, 128)
             top = jnp.max(h, axis=0)
@@ -199,14 +201,15 @@
             beta[b, t] = jnp.sum(e, axis=0)
         return carry
 
-    lax.fori_loop(0, CUTS, first_column, 0)
+    for b in range(CUTS):
+        first_column(b, 0)
     for t in range(TILES):
         cut_peak = gain[:, t]
         top = jnp.max(jnp.max(cut_peak, axis=0), axis=0, keepdims=True)
         sums = jnp.sum(jnp.sum(beta[:, t] * jnp.exp2(cut_peak - top), axis=0), axis=0, keepdims=True)
-        col_box[0, me, t:t + 1, :] = top + log2(sums)
+        col_box[me, t:t + 1, :] = top + log2(sums)
     col_trade(0)
-    col_log = -math.log2(COLS) - log_sum(col_box[0])
+    col_log = -math.log2(COLS) - log_sum(col_box[...])
     for t in range(TILES):
         start_gain = jnp.exp2(gain[:, t] + col_log[t:t + 1, :])
         gain[:, t] = start_gain
@@ -236,10 +239,10 @@
                 term = score[t // 2, r, lanes_of(t)] * weight
                 term = jnp.sum(term.reshape(CUT // 8, 8, 128), axis=0) * gain[b, t]
                 sums[t] = term if b == 0 else sums[t] + term
-        for t in range(TILES):
-            col_box[turn, me, t:t + 1, :] = jnp.sum(sums[t], axis=0, keepdims=True)
+        sums = [jnp.sum(part, axis=0, keepdims=True) for part in sums]
+        sum_box[turn - 1, me] = jnp.concatenate(sums, axis=0).astype(BF16)
         col_trade(turn)
-        factor = 1.0 / (COLS * jnp.sum(col_box[turn], axis=0))
+        factor = 1.0 / (COLS * jnp.sum(sum_box[turn - 1].astype(F32), axis=0))
         for t in range(TILES):
             beta[:, t] = gain[:, t] * factor[t:t + 1, :]
 
@@ -314,7 +317,7 @@
         wait(row_box.at[turn, 0:NZ - 1], s_row.at[turn])
         wait(core_box.at[turn, c], s_core.at[turn])
     for turn in range(ITERS):
-        wait(col_box.at[turn, 0:GROUP - 1], s_col.at[turn])
+        wait((col_box if turn == 0 else sum_box.at[turn - 1]).at[0:GROUP - 1], s_col.at[turn])
     wait(row_pot.at[0:NY - 1], s_rpot.at[0])
     wait(col_pot.at[c], s_cpot.at[0])
     for group in range(2):
@@ -358,7 +361,8 @@
             pltpu.VMEM((4 * SHARE, PIECES * PIECE), BF16),
             pltpu.VMEM((ITERS + 1, NZ, 8, 128), F32),
             pltpu.VMEM((ITERS + 1, NC, 8, 128), F32),
-            pltpu.VMEM((ITERS, GROUP, TILES, 128), F32),
+            pltpu.VMEM((GROUP, TILES, 128), F32),
+            pltpu.VMEM((ITERS - 1, GROUP, TILES, 128), BF16),
             pltpu.VMEM((NY, 8, 128), F32),
             pltpu.VMEM((NC, TILES, 128), F32),
             pltpu.VMEM((2, 8, 128), F32),

time: 75.7 us -> 74.2 us (0.980)
  Pallas kernels: 74.9 us -> 73.4 us
    pallas_call x1, Pallas kernels: 74.2 us -> 72.7 us  [shards(): pl.pallas_call(kernel, out_shape=shapes, in_specs=[hbm, hbm], out_specs=(...]
where the time goes in v4:
time: 74.2 us; the launch traced here: 74 us
  Pallas kernels  73.4 us (99%)
    pallas_call x1, Pallas kernels, shards(): pl.pallas_call(kernel, out_shape=shapes, in_specs=[hbm, hbm], out_specs=(...  72.7 us

profile of v4, /device:TPU:1, one launch (start us, length us, event | category | flops | bytes accessed | tf_op | source)
XLA Modules:
  0.0 74.0 jit_solution(11469193427721891356)
XLA Ops:
  0.6 72.7 %sinkhorn.1 = (f32[16,128]{1,0:T(8,128)S(1)}, f32[8,128]{1,0:T(8,128)S(1)}, bf16[64,256]{1,0:T(8,128)(2,1)S(1)}) custom-call(bf16[64,256]{1,0:T(8,128)(2,1)} %noise_hbm.1, bf16[32,1024]{1,0:T(8,128)(2,1)} %bitcast.3), custom_call_target="tpu_custom_call" | custom-call | tf_op jit(solution)/shard_map/sinkhorn/pallas_call | solution.py:346
  73.4 0.7 give.1

commit v5 on v4

--- a/solution.py
+++ b/solution.py
@@ -40,7 +40,7 @@
     return slice((t % 2) * 128, (t % 2) * 128 + 128)
 
 
-def kernel(noise_hbm, teach_hbm, row_out, col_out, target_out, offer, cols, rows_x, tall, score, peak, total,
+def kernel(noise_hbm, teach_hbm, row_out, col_out, target_out, offer, cols, rows_x, norms, tall, score, peak, total,
            gain, beta, plan, row_box, core_box, col_box, sum_box, row_pot, col_pot, mine, gifts, boxes,
            load, s_offer, r_offer, s_x, s_y, r_x, r_y, s_xy, s_yx, r_xy, r_yx, s_rows, r_rows, s_pair, r_pair,
            s_row, r_row, s_core, r_core, s_col, r_col, s_rpot, r_rpot, s_cpot, r_cpot, s_gift, r_gift, s_box, r_box):
@@ -56,9 +56,11 @@
     across = [py * NZ + z for py in ys]
     along = [y * NZ + pz for pz in zs]
     sibling = (x * NC + other, s)
-    xy = [(noise_at[k // NY], across[k % NY]) for k in range(1, GROUP)]
     ring = [1, 3, 2]
     near = [1, 7, 2, 6, 3, 5, 4]
+    far = near[::-1]
+    corner = sorted(range(1, GROUP), key=lambda k: -(min(k // NY, NX - k // NY) + min(k % NY, NY - k % NY)))
+    xy = [(noise_at[k // NY], across[k % NY]) for k in corner]
 
     def send(src, dst, send_sem, recv_sem, device):
         pltpu.make_async_remote_copy(src_ref=src, dst_ref=dst, send_sem=send_sem, recv_sem=recv_sem,
@@ -94,7 +96,7 @@
         send(own, own, s_x.at[0], r_xy.at[y], (n, across[d]))
     for d in near:
         send(rows_x.at[z, c], rows_x.at[z, c], s_rows.at[0], r_rows.at[z], (n, along[d]))
-    send(rows_x.at[z, c], rows_x.at[z, c], s_pair.at[0], r_pair.at[0], sibling)
+    send(rows_x.at[z, c], rows_x.at[z, c], s_pair.at[0], r_pair.at[z], sibling)
     wait(theirs, r_offer.at[0])
     for d in ring:
         send(theirs, theirs, s_y.at[0], r_y.at[y], (n, across[d]))
@@ -109,46 +111,65 @@
         wait(passed, r_y.at[ys[q]])
         for e in ring:
             send(passed, passed, s_yx.at[0], r_yx.at[ys[q]], (noise_at[e], s))
-    for d in near:
-        passed = rows_x.at[zs[d], c]
-        wait(passed, r_rows.at[zs[d]])
-        send(passed, passed, s_pair.at[0], r_pair.at[0], sibling)
-    wait(rows_x.at[:, other], r_pair.at[0])
-
     def block_of(py, part):
         return cols[py, :, :, :, part * PIECE:(part + 1) * PIECE].reshape(WIDTH, PIECE)
 
-    def scores_of(py, part):
-        block = block_of(py, part)
-        wide = block.astype(F32)
-        norms = jnp.sum(wide * wide, axis=0, keepdims=True) * (COST / LN2)
-        for b in range(CUTS):
-            r = slice(b * CUT, (b + 1) * CUT)
-            dots = jnp.dot(rows_x[b].reshape(CUT, WIDTH), block, preferred_element_type=F32)
-            h = dots * (2.0 * COST / LN2) - norms
-            score[py * 2 + part, r, :] = h
-            left, right = h[:, :128], h[:, 128:]
+    def norms_of(py):
+        for part in range(2):
+            wide = block_of(py, part).astype(F32)
+            norms[py * 2 + part] = jnp.sum(wide * wide, axis=0, keepdims=True) * (COST / LN2)
+
+    def scores_of(py, blocks):
+        for b in blocks:
+            r = slice(b * CUT, (b + 1) * CUT) if isinstance(b, int) else pl.ds(pl.multiple_of(b * CUT, CUT), CUT)
+            latents = rows_x[b].reshape(CUT, WIDTH)
+            tiles = []
+            for part in range(2):
+                dots = jnp.dot(latents, block_of(py, part), preferred_element_type=F32)
+                h = dots * (2.0 * COST / LN2) - norms[py * 2 + part]
+                score[py * 2 + part, r, :] = h
+                tiles += [h[:, :128], h[:, 128:]]
             old = peak[r, :]
-            new = jnp.maximum(old, jnp.maximum(left, right))
-            total[r, :] = total[r, :] * jnp.exp2(old - new) + (jnp.exp2(left - new) + jnp.exp2(right - new))
+            new = jnp.maximum(jnp.maximum(tiles[0], tiles[1]), jnp.maximum(tiles[2], tiles[3]))
+            new = jnp.maximum(old, new)
+            sums = [jnp.exp2(tile - new) for tile in tiles]
+            total[r, :] = total[r, :] * jnp.exp2(old - new) + ((sums[0] + sums[1]) + (sums[2] + sums[3]))
             peak[r, :] = new
+
+    def piece_wait(py):
+        wait(cols.at[py, :, c], r_xy.at[py])
+        wait(cols.at[py, 0:NX - 1, other], r_yx.at[py])
+        norms_of(py)
+
+    def off(k):
+        return lax.rem(z + lax.div(k + 1, 2) * (2 * lax.rem(k, 2) - 1) + NZ, NZ)
+
+    wait(cols.at[y, 0:NX - 1, other], r_yx.at[y])
+    norms_of(y)
+
+    def rows_in(k, carry):
+        pz, last = off(k), off(k - 1)
+        passed = rows_x.at[pz, c]
+        wait(passed, r_rows.at[pz])
+        send(passed, passed, s_pair.at[0], r_pair.at[pz], sibling)
+        wait(rows_x.at[last, other], r_pair.at[last])
+        scores_of(y, [last])
+        return carry
+
+    lax.fori_loop(1, NZ, rows_in, 0)
+    wait(rows_x.at[zs[4], other], r_pair.at[zs[4]])
+    scores_of(y, [zs[4]])
 
     def piece(k, carry):
         py = lax.rem(y + lax.div(3 * k * (k + 1), 2), NY)
-
-        @pl.when(k > 0)
-        def _():
-            wait(cols.at[py, :, c], r_xy.at[py])
-
-        wait(cols.at[py, 0:NX - 1, other], r_yx.at[py])
-        scores_of(py, 0)
-        scores_of(py, 1)
+        piece_wait(py)
+        scores_of(py, range(CUTS))
         return carry
 
-    lax.fori_loop(0, NY, piece, 0)
+    lax.fori_loop(1, NY, piece, 0)
 
     def row_start(turn):
-        for d in near:
+        for d in far:
             send(row_box.at[turn, z], row_box.at[turn, z], s_row.at[turn], r_row.at[turn], (n, along[d]))
 
     def row_wait(turn):
@@ -352,6 +373,7 @@
             pltpu.VMEM((FEATURES, HALF), BF16),
             pltpu.VMEM((NY, NX, NC, FEATURES, HALF), BF16),
             pltpu.VMEM((NZ, NC, SHARE, WIDTH), BF16),
+            pltpu.VMEM((PIECES, 1, PIECE), F32),
             pltpu.VMEM((PIECES * PIECE, WIDTH), BF16),
             pltpu.VMEM((PIECES, BLOCK_ROWS, PIECE), F32),
             pltpu.VMEM((BLOCK_ROWS, 128), F32),
@@ -373,7 +395,7 @@
             dma((1,)), dma((1,)), dma((NX,)), dma((NY,)),
             dma((1,)), dma((1,)), dma((NY,)), dma((NY,)),
             dma((1,)), dma((NZ,)),
-            dma((1,)), dma((1,)),
+            dma((1,)), dma((NZ,)),
             dma((ITERS + 1,)), dma((ITERS + 1,)),
             dma((ITERS + 1,)), dma((ITERS + 1,)),
             dma((ITERS,)), dma((ITERS,)),

time: 74.2 us -> 72.4 us (0.976)
  Pallas kernels: 73.4 us -> 71.6 us
    pallas_call x1, Pallas kernels: 72.7 us -> 70.9 us  [shards(): pl.pallas_call(kernel, out_shape=shapes, in_specs=[hbm, hbm], out_specs=(...]
where the time goes in v5:
time: 72.4 us; the launch traced here: 72.2 us
  Pallas kernels  71.6 us (99%)
    pallas_call x1, Pallas kernels, shards(): pl.pallas_call(kernel, out_shape=shapes, in_specs=[hbm, hbm], out_specs=(...  70.9 us

profile of v5, /device:TPU:1, one launch (start us, length us, event | category | flops | bytes accessed | tf_op | source)
XLA Modules:
  0.0 72.2 jit_solution(8952204616990195126)
XLA Ops:
  0.6 70.9 %sinkhorn.1 = (f32[16,128]{1,0:T(8,128)S(1)}, f32[8,128]{1,0:T(8,128)S(1)}, bf16[64,256]{1,0:T(8,128)(2,1)S(1)}) custom-call(bf16[64,256]{1,0:T(8,128)(2,1)} %noise_hbm.1, bf16[32,1024]{1,0:T(8,128)(2,1)} %bitcast.3), custom_call_target="tpu_custom_call" | custom-call | tf_op jit(solution)/shard_map/sinkhorn/pallas_call | solution.py:367
  71.5 0.7 give.1

commit v6 on v5

--- a/solution.py
+++ b/solution.py
@@ -81,7 +81,7 @@
         copy.start()
 
     barrier = pltpu.get_barrier_semaphore()
-    greeted = xy + [(n, along[d]) for d in range(1, NZ)] + [sibling]
+    greeted = xy[:1] + [(n, along[d]) for d in far] + xy[1:] + [sibling]
     for device in greeted:
         pl.semaphore_signal(barrier, inc=1, device_id=device, device_id_type=MESH)
     peak[...] = jnp.full((BLOCK_ROWS, 128), -1e30, F32)
@@ -236,15 +236,19 @@
         gain[:, t] = start_gain
         beta[:, t] = start_gain
 
-    alpha = None
-    for turn in range(1, ITERS):
+    def row_sums_into(turn, scale):
         for b in range(CUTS):
             r = slice(b * CUT, (b + 1) * CUT)
             acc = None
             for t in range(TILES):
                 term = score[t // 2, r, lanes_of(t)].reshape(CUT // 8, 8, 128) * beta[b, t]
                 acc = term if acc is None else acc + term
-            row_box[turn, z, b:b + 1, :] = jnp.sum(acc.reshape(CUT, 128).T, axis=0, keepdims=True)
+            sums = jnp.sum(acc.reshape(CUT, 128).T, axis=0, keepdims=True)
+            row_box[turn, z, b:b + 1, :] = sums if scale is None else sums * scale[b:b + 1, :]
+
+    alpha = None
+    for turn in range(1, ITERS):
+        row_sums_into(turn, None)
         row_start(turn)
         row_wait(turn)
         pair = core_trade(turn, jnp.sum(row_box[turn], axis=0))
@@ -274,14 +278,13 @@
             pz = zs[order[4 * group + k]]
             r = pl.ds(pl.multiple_of(pz * CUT + which * SHARE, SHARE), SHARE)
             weight = total[r, :]
-            acc = None
             for t in range(TILES):
                 p = (score[t // 2, r, lanes_of(t)] * weight).reshape(SHARE // 8, 8, 128) * beta[pz, t]
-                acc = p if acc is None else acc + p
                 plan[k * SHARE:(k + 1) * SHARE, t * 128:t * 128 + 128] = p.reshape(SHARE, 128).astype(BF16)
-            peak[r, :] = acc.reshape(SHARE, 128)
         return jnp.dot(plan[...], tall[...], preferred_element_type=F32)
 
+    row_sums_into(ITERS, alpha)
+    row_start(ITERS)
     for group in range(2):
         gifts[0, group] = project(other, group).astype(BF16)
         send(gifts.at[0, group], gifts.at[1, group], s_gift.at[group], r_gift.at[group], sibling)
@@ -295,9 +298,6 @@
             if d:
                 send(boxes.at[0, d], boxes.at[1, z], s_box.at[0], r_box.at[0], (n, along[d]))
     boxes[1, z] = boxes[0, 0]
-    for b in range(CUTS):
-        row_box[ITERS, z, b:b + 1, :] = jnp.sum(peak[b * CUT:(b + 1) * CUT, :].T, axis=0, keepdims=True)
-    row_start(ITERS)
 
     row_pot[y] = COST * mine[0] + LN2 * (row_log + log2(alpha))
     col_pot[c] = LN2 * (col_log + log2(factor))

time: 72.4 us -> 69.7 us (0.963)
  Pallas kernels: 71.6 us -> 68.9 us
    pallas_call x1, Pallas kernels: 70.9 us -> 68.2 us  [shards(): pl.pallas_call(kernel, out_shape=shapes, in_specs=[hbm, hbm], out_specs=(...]
where the time goes in v6:
time: 69.7 us; the launch traced here: 69.5 us
  Pallas kernels  68.9 us (99%)
    pallas_call x1, Pallas kernels, shards(): pl.pallas_call(kernel, out_shape=shapes, in_specs=[hbm, hbm], out_specs=(...  68.2 us

profile of v6, /device:TPU:1, one launch (start us, length us, event | category | flops | bytes accessed | tf_op | source)
XLA Modules:
  0.0 69.5 jit_solution(15395586680128012244)
XLA Ops:
  0.6 68.2 %sinkhorn.1 = (f32[16,128]{1,0:T(8,128)S(1)}, f32[8,128]{1,0:T(8,128)S(1)}, bf16[64,256]{1,0:T(8,128)(2,1)S(1)}) custom-call(bf16[64,256]{1,0:T(8,128)(2,1)} %noise_hbm.1, bf16[32,1024]{1,0:T(8,128)(2,1)} %bitcast.3), custom_call_target="tpu_custom_call" | custom-call | tf_op jit(solution)/shard_map/sinkhorn/pallas_call | solution.py:367
  68.8 0.7 give.1

commit v7 on v6

--- a/solution.py
+++ b/solution.py
@@ -283,13 +283,11 @@
                 plan[k * SHARE:(k + 1) * SHARE, t * 128:t * 128 + 128] = p.reshape(SHARE, 128).astype(BF16)
         return jnp.dot(plan[...], tall[...], preferred_element_type=F32)
 
-    row_sums_into(ITERS, alpha)
-    row_start(ITERS)
-    for group in range(2):
+    def give_to_sibling(group):
         gifts[0, group] = project(other, group).astype(BF16)
         send(gifts.at[0, group], gifts.at[1, group], s_gift.at[group], r_gift.at[group], sibling)
-    for group in range(2):
-        numer = project(c, group)
+
+    def give_along(group, numer):
         wait(gifts.at[1, group], r_gift.at[group])
         numer = (numer + gifts[1, group].astype(F32)).astype(BF16)
         for k in range(4):
@@ -297,6 +295,14 @@
             boxes[0, d] = numer[k * SHARE:(k + 1) * SHARE, :]
             if d:
                 send(boxes.at[0, d], boxes.at[1, z], s_box.at[0], r_box.at[0], (n, along[d]))
+
+    give_to_sibling(0)
+    row_sums_into(ITERS, alpha)
+    row_start(ITERS)
+    first = project(c, 0)
+    give_along(0, first)
+    give_to_sibling(1)
+    give_along(1, project(c, 1))
     boxes[1, z] = boxes[0, 0]
 
     row_pot[y] = COST * mine[0] + LN2 * (row_log + log2(alpha))

time: 69.7 us -> 69.4 us (level)
  no operation moved by 1% of the time
where the time goes in v7:
time: 69.4 us; the launch traced here: 69.2 us
  Pallas kernels  68.6 us (99%)
    pallas_call x1, Pallas kernels, shards(): pl.pallas_call(kernel, out_shape=shapes, in_specs=[hbm, hbm], out_specs=(...  67.9 us

profile of v7, /device:TPU:1, one launch (start us, length us, event | category | flops | bytes accessed | tf_op | source)
XLA Modules:
  0.0 69.2 jit_solution(7300740096720030030)
XLA Ops:
  0.6 67.9 %sinkhorn.1 = (f32[16,128]{1,0:T(8,128)S(1)}, f32[8,128]{1,0:T(8,128)S(1)}, bf16[64,256]{1,0:T(8,128)(2,1)S(1)}) custom-call(bf16[64,256]{1,0:T(8,128)(2,1)} %noise_hbm.1, bf16[32,1024]{1,0:T(8,128)(2,1)} %bitcast.3), custom_call_target="tpu_custom_call" | custom-call | tf_op jit(solution)/shard_map/sinkhorn/pallas_call | solution.py:373
  68.5 0.7 give.1
